TPU v7x, 32 devices: a whole 2x2x4 slice. The times are simulated.
32 devices in a mesh: dp: 8 (over y, x, core), tensor: 4 (over z).
Axes of the slice: x: 2, y: 2, z: 4, core: 2. Of those that a mesh axis runs over, the one named last changes fastest.
Arguments:
- tokens: bfloat16 [16384, 1024], P(('dp', 'tensor')), may hold values from -6 to 6
- w_qkv: bfloat16 [3, 1024, 1024], P(None, 'dp', 'tensor'), may hold values from -0.1875 to 0.1875
- w_attn_out: bfloat16 [1024, 1024], P('dp', 'tensor'), may hold values from -1.5 to 1.5
- w_in: bfloat16 [1024, 4096], P('dp', 'tensor'), may hold values from -0.1875 to 0.1875
- w_out: bfloat16 [1024, 4096], P('dp', 'tensor'), may hold values from -0.09375 to 0.09375
- b_qv: bfloat16 [2, 1024], P(None, 'dp'), may hold values from -0.59765625 to 0.59765625
- b_proj: bfloat16 [2, 1024], P(None, 'dp'), may hold values from -3 to 3
- b_hidden: bfloat16 [4096], P('dp'), may hold values from -3 to 3
- ln_gain: bfloat16 [2, 1024], P(None, 'dp'), may hold values from 0.25 to 1.75
- ln_bias: bfloat16 [2, 1024], P(None, 'dp'), may hold values from -2 to 2
- doc_lengths: int32 [8, 4], P('dp'), may hold values from 1 to 1600, 2048 in all within a row
- cotangent: bfloat16 [16384, 1024], P(('dp', 'tensor')), may hold values from -6 to 6
Outputs:
- output: bfloat16 [16384, 1024], P(('dp', 'tensor'))
- grad_tokens: bfloat16 [16384, 1024], P(('dp', 'tensor'))
- grad_qkv: float32 [3, 1024, 1024], P(None, 'dp', 'tensor')
- grad_attn_out: float32 [1024, 1024], P('dp', 'tensor')
- grad_in: float32 [1024, 4096], P('dp', 'tensor')
- grad_out: float32 [1024, 4096], P('dp', 'tensor')
- grad_qv: float32 [2, 1024], P(None, 'dp')
- grad_proj: float32 [2, 1024], P(None, 'dp')
- grad_hidden: float32 [4096], P('dp')
- grad_gain: float32 [2, 1024], P(None, 'dp')
- grad_shift: float32 [2, 1024], P(None, 'dp')
Inputs may be any that keep to these rules, and one draw needn't show every extreme that they name: `doc_lengths`: row s holds the lengths of the 4 documents packed into sequence s, in order; they sum to 2048, and the longest of each row is exactly 1600.
All inputs are finite; a program needn't handle non-finite values.
Results may differ from a plain program's by a relative error of at most 0.02.
Values may be sent and summed in bfloat16 or wider, within the bound.
A program may use at most 128 MiB of HBM per device.

v0:
```python
import jax
import jax.numpy as jnp
from jax import lax
from jax.sharding import PartitionSpec as P

HD = 64
LEN = 2048


epsilon = 1e-06


def layer_norm(rows, gain, shift):
    centred = rows - jnp.mean(rows, -1, keepdims=True)
    spread = jnp.mean(centred * centred, -1, keepdims=True)
    return centred * lax.rsqrt(spread + epsilon) * gain + shift


def gelu_exact(values):
    return jax.nn.gelu(values, approximate=False)


def segment_ids(lengths, length):
    ends = jnp.cumsum(lengths, axis=-1)
    places = jnp.arange(length, dtype=jnp.int32)
    return jnp.sum((places[None, :, None] >= ends[:, None, :]).astype(jnp.int32), -1)


def matmul(left, right):
    return jnp.dot(left, right, preferred_element_type=jnp.float32)


def matmul_nt(left, right):
    return lax.dot_general(
        left, right, (((1,), (1,)), ((), ())), preferred_element_type=jnp.float32
    )


def matmul_tn(left, right):
    return lax.dot_general(
        left, right, (((0,), (0,)), ((), ())), preferred_element_type=jnp.float32
    )


def attend_forward(queries, keys, values, segments, head_dim, block):
    seqs, length, local = queries.shape
    heads = local // head_dim
    blocks = length // block
    scale = head_dim ** (-0.5)

    def attend_one_block(index):
        seq_index = index // (heads * blocks)
        head_index = index // blocks % heads
        block_index = index % blocks
        query_rows = lax.dynamic_slice(
            queries, (seq_index, block_index * block, head_index * head_dim), (1, block, head_dim)
        )[0]
        key_rows = lax.dynamic_slice(
            keys, (seq_index, 0, head_index * head_dim), (1, length, head_dim)
        )[0]
        value_rows = lax.dynamic_slice(
            values, (seq_index, 0, head_index * head_dim), (1, length, head_dim)
        )[0]
        seg_all = segments[0]
        seg_query = lax.dynamic_slice_in_dim(seg_all, block_index * block, block, 0)
        scores = matmul_nt(query_rows, key_rows) * scale
        scores = jnp.where(seg_query[:, None] == seg_all[None, :], scores, -jnp.inf)
        peaks = jnp.max(scores, -1, keepdims=True)
        powered = jnp.exp(scores - peaks)
        totals = jnp.sum(powered, -1, keepdims=True)
        weights = powered / totals
        context = matmul(weights.astype(jnp.bfloat16), value_rows)
        return (context, (peaks + jnp.log(totals))[:, 0])

    contexts, log_sums = lax.map(
        attend_one_block, jnp.arange(seqs * heads * blocks, dtype=jnp.int32)
    )
    contexts = (
        contexts.reshape(seqs, heads, blocks, block, head_dim)
        .transpose(0, 2, 3, 1, 4)
        .reshape(seqs * length, local)
    )
    return (contexts, log_sums)


def attend_backward(queries, keys, values, segments, log_sums, grad_context, head_dim, block):
    seqs, length, local = queries.shape
    heads = local // head_dim
    blocks = length // block
    scale = head_dim ** (-0.5)
    sums_table = log_sums.reshape(seqs * heads, blocks, block)

    def one_head(index):
        seq_index = index // heads
        head_index = index % heads
        corner = (seq_index, 0, head_index * head_dim)
        extent = (1, length, head_dim)
        key_rows = lax.dynamic_slice(keys, corner, extent)[0]
        value_rows = lax.dynamic_slice(values, corner, extent)[0]
        query_all = lax.dynamic_slice(queries, corner, extent)[0]
        grad_all = lax.dynamic_slice(grad_context, corner, extent)[0]
        seg_all = segments[0]
        head_sums = lax.dynamic_slice_in_dim(sums_table, index, 1, 0)[0]

        def one_one_block(carry, block_index):
            grad_keys, grad_values = carry
            query_rows = lax.dynamic_slice_in_dim(query_all, block_index * block, block, 0)
            grad_rows = lax.dynamic_slice_in_dim(grad_all, block_index * block, block, 0)
            seg_query = lax.dynamic_slice_in_dim(seg_all, block_index * block, block, 0)
            log_rows = lax.dynamic_slice_in_dim(head_sums, block_index, 1, 0)[0]
            scores = matmul_nt(query_rows, key_rows) * scale
            scores = jnp.where(seg_query[:, None] == seg_all[None, :], scores, -jnp.inf)
            weights = jnp.exp(scores - log_rows[:, None])
            grad_weights = matmul_nt(grad_rows, value_rows)
            inner = jnp.sum(grad_weights * weights, -1, keepdims=True)
            grad_scores = (weights * (grad_weights - inner)).astype(jnp.bfloat16)
            grad_queries = matmul(grad_scores, key_rows) * scale
            grad_keys = grad_keys + matmul_tn(grad_scores, query_rows) * scale
            grad_values = grad_values + matmul_tn(weights.astype(jnp.bfloat16), grad_rows)
            return ((grad_keys, grad_values), grad_queries)

        zeros = jnp.zeros((length, head_dim), jnp.float32)
        (grad_keys, grad_values), grad_queries = lax.scan(
            one_one_block, (zeros, zeros), jnp.arange(blocks, dtype=jnp.int32)
        )
        return (grad_queries.reshape(length, head_dim), grad_keys, grad_values)

    results = lax.map(one_head, jnp.arange(seqs * heads, dtype=jnp.int32))
    return tuple(
        (
            array.reshape(seqs, heads, length, head_dim)
            .transpose(0, 2, 1, 3)
            .reshape(seqs * length, local)
            .astype(jnp.bfloat16)
            for array in results
        )
    )


def column_sum(array):
    return jnp.sum(array.astype(jnp.float32), 0)


def on_device(
    tokens,
    w_qkv,
    w_attn_out,
    w_in,
    w_out,
    b_qv,
    b_proj,
    b_hidden,
    ln_gain,
    ln_bias,
    doc_lengths,
    cotangent,
):
    head_dim = HD
    rows_here, width = tokens.shape
    members = lax.axis_size("tensor")
    group_rows = rows_here * members
    seqs = group_rows // LEN
    block = min(512, LEN)
    position = lax.axis_index("tensor")
    qkv_all, attn_out_all, in_all, out_all, qv_bias, proj_bias, hidden_bias, gains, shifts = (
        lax.all_gather(w_qkv, "dp", axis=1, tiled=True),
        lax.all_gather(w_attn_out, "dp", axis=0, tiled=True),
        lax.all_gather(w_in, "dp", axis=0, tiled=True),
        lax.all_gather(w_out, "dp", axis=0, tiled=True),
        lax.all_gather(b_qv, "dp", axis=1, tiled=True),
        lax.all_gather(b_proj, "dp", axis=1, tiled=True),
        lax.all_gather(b_hidden, "dp", axis=0, tiled=True),
        lax.all_gather(ln_gain, "dp", axis=1, tiled=True),
        lax.all_gather(ln_bias, "dp", axis=1, tiled=True),
    )
    local = qkv_all.shape[2]
    hidden_local = in_all.shape[1]
    qv_bias = qv_bias.astype(jnp.float32)
    proj_bias = proj_bias.astype(jnp.float32)
    gains = gains.astype(jnp.float32)
    shifts = shifts.astype(jnp.float32)
    query_bias = lax.dynamic_slice_in_dim(qv_bias[0], position * local, local)
    value_bias = lax.dynamic_slice_in_dim(qv_bias[1], position * local, local)
    hidden_here = lax.dynamic_slice_in_dim(
        hidden_bias.astype(jnp.float32), position * hidden_local, hidden_local
    )
    segments = segment_ids(doc_lengths, LEN)
    shape_three = (seqs, LEN, local)
    inputs = lax.all_gather(tokens, "tensor", axis=0, tiled=True)
    queries = (matmul(inputs, qkv_all[0]) + query_bias).astype(jnp.bfloat16)
    keys = matmul(inputs, qkv_all[1]).astype(jnp.bfloat16)
    values = (matmul(inputs, qkv_all[2]) + value_bias).astype(jnp.bfloat16)
    context, log_sums = attend_forward(
        queries.reshape(shape_three),
        keys.reshape(shape_three),
        values.reshape(shape_three),
        segments,
        head_dim,
        block,
    )
    context = context.astype(jnp.bfloat16)
    attended = (
        lax.psum_scatter(
            matmul_nt(context, attn_out_all).astype(jnp.bfloat16),
            "tensor",
            scatter_dimension=0,
            tiled=True,
        ).astype(jnp.float32)
        + proj_bias[0]
    )
    normed_one, norm_one_pull = jax.vjp(
        layer_norm, tokens.astype(jnp.float32) + attended, gains[0], shifts[0]
    )
    normed_all = lax.all_gather(normed_one.astype(jnp.bfloat16), "tensor", axis=0, tiled=True)
    hidden_pre = matmul(normed_all, in_all) + hidden_here
    activated, gelu_pull = jax.vjp(gelu_exact, hidden_pre)
    activated = activated.astype(jnp.bfloat16)
    mixed = (
        lax.psum_scatter(
            matmul_nt(activated, out_all).astype(jnp.bfloat16),
            "tensor",
            scatter_dimension=0,
            tiled=True,
        ).astype(jnp.float32)
        + proj_bias[1]
    )
    output, norm_two_pull = jax.vjp(layer_norm, normed_one + mixed, gains[1], shifts[1])
    qkv_all, attn_out_all, in_all, out_all = (
        lax.all_gather(w_qkv, "dp", axis=1, tiled=True),
        lax.all_gather(w_attn_out, "dp", axis=0, tiled=True),
        lax.all_gather(w_in, "dp", axis=0, tiled=True),
        lax.all_gather(w_out, "dp", axis=0, tiled=True),
    )
    grad_two, gain_two, shift_two = norm_two_pull(cotangent.astype(jnp.float32))
    grad_mixed = grad_two.astype(jnp.bfloat16)
    grad_mixed_all = lax.all_gather(grad_mixed, "tensor", axis=0, tiled=True)
    grad_act = matmul(grad_mixed_all, out_all)
    grad_pre = gelu_pull(grad_act)[0].astype(jnp.bfloat16)
    grad_in_part = matmul_tn(normed_all, grad_pre)
    grad_out_part = matmul_tn(grad_mixed_all, activated)
    grad_in, grad_out = (
        lax.psum_scatter(grad_in_part, "dp", scatter_dimension=0, tiled=True),
        lax.psum_scatter(grad_out_part, "dp", scatter_dimension=0, tiled=True),
    )
    grad_normed = (
        lax.psum_scatter(
            matmul_nt(grad_pre, in_all).astype(jnp.bfloat16),
            "tensor",
            scatter_dimension=0,
            tiled=True,
        ).astype(jnp.float32)
        + grad_two
    )
    grad_one, gain_one, shift_one = norm_one_pull(grad_normed)
    grad_attended = grad_one.astype(jnp.bfloat16)
    grad_att_all = lax.all_gather(grad_attended, "tensor", axis=0, tiled=True)
    grad_context = matmul(grad_att_all, attn_out_all).astype(jnp.bfloat16)
    grad_attn_part = matmul_tn(grad_att_all, context)
    grad_queries, grad_keys, grad_values = attend_backward(
        queries.reshape(shape_three),
        keys.reshape(shape_three),
        values.reshape(shape_three),
        segments,
        log_sums,
        grad_context.reshape(shape_three),
        head_dim,
        block,
    )
    grad_qkv_part = jnp.stack(
        [
            matmul_tn(inputs, grad_queries),
            matmul_tn(inputs, grad_keys),
            matmul_tn(inputs, grad_values),
        ]
    )
    total = matmul_nt(grad_queries, qkv_all[0])
    total = total + matmul_nt(grad_keys, qkv_all[1])
    grad_tokens = (
        lax.psum_scatter(
            (total + matmul_nt(grad_values, qkv_all[2])).astype(jnp.bfloat16),
            "tensor",
            scatter_dimension=0,
            tiled=True,
        ).astype(jnp.float32)
        + grad_one
    ).astype(jnp.bfloat16)

    def placed(piece, full):
        return lax.dynamic_update_slice_in_dim(
            jnp.zeros((full,), jnp.float32), piece, position * piece.shape[0], 0
        )

    qv_part = jnp.stack(
        [placed(column_sum(grad_queries), width), placed(column_sum(grad_values), width)]
    )
    proj_part = jnp.stack([column_sum(grad_attended), column_sum(grad_mixed)])
    hidden_part = placed(column_sum(grad_pre), hidden_local * members)
    gain_part = jnp.stack([gain_one, gain_two])
    shift_part = jnp.stack([shift_one, shift_two])
    qv_sum, proj_sum, hidden_sum, gain_sum, shift_sum = (
        lax.psum(qv_part.astype(jnp.bfloat16), "tensor").astype(jnp.float32),
        lax.psum(proj_part.astype(jnp.bfloat16), "tensor").astype(jnp.float32),
        lax.psum(hidden_part.astype(jnp.bfloat16), "tensor").astype(jnp.float32),
        lax.psum(gain_part.astype(jnp.bfloat16), "tensor").astype(jnp.float32),
        lax.psum(shift_part.astype(jnp.bfloat16), "tensor").astype(jnp.float32),
    )
    grad_qkv, grad_attn_out, grad_qv, grad_proj, grad_hidden, grad_gain, grad_shift = (
        lax.psum_scatter(grad_qkv_part, "dp", scatter_dimension=1, tiled=True),
        lax.psum_scatter(grad_attn_part, "dp", scatter_dimension=0, tiled=True),
        lax.psum_scatter(qv_sum, "dp", scatter_dimension=1, tiled=True),
        lax.psum_scatter(proj_sum, "dp", scatter_dimension=1, tiled=True),
        lax.psum_scatter(hidden_sum, "dp", scatter_dimension=0, tiled=True),
        lax.psum_scatter(gain_sum, "dp", scatter_dimension=1, tiled=True),
        lax.psum_scatter(shift_sum, "dp", scatter_dimension=1, tiled=True),
    )
    return (
        output.astype(jnp.bfloat16),
        grad_tokens,
        grad_qkv,
        grad_attn_out,
        grad_in,
        grad_out,
        grad_qv,
        grad_proj,
        grad_hidden,
        grad_gain,
        grad_shift,
    )


def solution(mesh):
    in_specs = (
        P(("dp", "tensor"), None),
        P(None, "dp", "tensor"),
        P("dp", "tensor"),
        P("dp", "tensor"),
        P("dp", "tensor"),
        P(None, "dp"),
        P(None, "dp"),
        P("dp"),
        P(None, "dp"),
        P(None, "dp"),
        P("dp", None),
        P(("dp", "tensor"), None),
    )
    out_specs = (
        P(("dp", "tensor"), None),
        P(("dp", "tensor"), None),
        P(None, "dp", "tensor"),
        P("dp", "tensor"),
        P("dp", "tensor"),
        P("dp", "tensor"),
        P(None, "dp"),
        P(None, "dp"),
        P("dp"),
        P(None, "dp"),
        P(None, "dp"),
    )
    return jax.shard_map(
        on_device, mesh=mesh, in_specs=in_specs, out_specs=out_specs, check_vma=False
    )
```

profile of v0, /device:TPU:0, one launch (start us, length us, event | category | flops | bytes accessed | tf_op | source)
XLA Modules:
  0.0 1631.4 jit_solution(6493453166586480195)
XLA Ops:
  9.6 10.3 all_gather.45
  20.0 10.2 all_gather.46
  30.2 8.7 all-gather.11.cloned.1.call-done
  38.8 82.4 %all-gather.9.cloned.1.call-done = bf16[2048,1024]{1,0:T(8,128)(2,1)} async-done(((bf16[512,1024]{1,0:T(8,128)(2,1)}), bf16[2048,1024]{1,0:T(8,128)(2,1)}) %all-gather.9.cloned.1.call-update) | async-done | bytes 4194320 | tf_op jit(solution)/shard_map/all_gather | solution.py:189
  121.2 4.7 fusion.35
  130.5 183.0 %while.60 = (s32[]{:T(128)}, bf16[16,512,64]{1,2,0:T(8,128)(2,1)S(1)}, f32[16,512]{1,0:T(8,128)S(1)}, s32[16]{0:T(128)S(1)}, s32[1,2048]{1,0:T(1,128)S(1)}, /*in...) while((s32[]{:T(128)}, ...), condition=%wide.region_5.6_spmd, body=%wide.region_2.5_spmd.sunk | while | flops 277872160 | bytes 30708316 | solution.py:75
  138.5 3.4 fusion.116
  150.0 3.4 fusion.116
  161.4 3.4 fusion.116
  172.8 3.4 fusion.116
  184.3 3.4 fusion.116
  195.7 3.4 fusion.116
  207.1 3.4 fusion.116
  218.6 3.4 fusion.116
  230.0 3.4 fusion.116
  241.4 3.4 fusion.116
  252.9 3.4 fusion.116
  264.3 3.4 fusion.116
  275.7 3.4 fusion.116
  287.2 3.4 fusion.116
  298.6 3.4 fusion.116
  310.1 3.4 fusion.116
  315.6 3.2 convolution_convert_fusion
  319.5 8.8 all_gather.47
  328.3 8.7 all_gather.48
  337.0 8.0 all_gather.49
  345.0 49.4 %reduce-scatter.21.cloned.1.call-done = bf16[512,1024]{1,0:T(8,128)(2,1)} async-done(((bf16[2048,1024]{1,0:T(8,128)(2,1)}), bf16[512,1024]{1,0:T(8,128)(2,1)}) %reduce-scatter.21.cloned.1.call-update) | async-done | bytes 1048592 | tf_op jit(solution)/shard_map/reduce_scatter | solution.py:203
  400.1 8.9 all-gather
  409.0 15.7 all-gather.15.cloned.1.call-done
  424.7 82.9 %all-gather.13.cloned.1.call-done = bf16[2048,1024]{1,0:T(8,128)(2,1)} async-done(((bf16[512,1024]{1,0:T(8,128)(2,1)}), bf16[2048,1024]{1,0:T(8,128)(2,1)}) %all-gather.13.cloned.1.call-update) | async-done | bytes 4194320 | tf_op jit(solution)/shard_map/all_gather | solution.py:214
  507.6 26.2 %multiply_convert_fusion.1 = (bf16[2048,1024]{1,0:T(8,128)(2,1)}, f32[2048,1024]{1,0:T(8,128)}, f32[2048,1024]{1,0:T(8,128)}) fusion(f32[1024]{0:T(1024)S(1)} %dynamic_slice.98, bf16[2048,1024]{1,0:T(8,128)(2,1)} %all-gather.13.cloned.1.call-done, bf16[1024,1024]{1,0:T(8,128)(2,1)} %all-gather.15.cloned.1.call-done), kind=kOutput, calls=%fused_computation.50 | convolution fusion | flops 4433379328 | bytes 27267072 | tf_op jit(solution)/shard_map/dot_general | solution.py:30
  535.9 9.4 convolution_convert_fusion.2
  545.8 76.4 %reduce-scatter.23.cloned.1.call-done = bf16[512,1024]{1,0:T(8,128)(2,1)} async-done(((bf16[2048,1024]{1,0:T(8,128)(2,1)}), bf16[512,1024]{1,0:T(8,128)(2,1)}) %reduce-scatter.23.cloned.1.call-update) | async-done | bytes 1048592 | tf_op jit(solution)/shard_map/reduce_scatter | solution.py:219
  630.1 81.4 %all-gather.19.cloned.1.call-done = bf16[2048,1024]{1,0:T(8,128)(2,1)} async-done(((bf16[512,1024]{1,0:T(8,128)(2,1)}), bf16[2048,1024]{1,0:T(8,128)(2,1)}) %all-gather.19.cloned.1.call-update) | async-done | bytes 4194320 | tf_op jit(solution)/shard_map/all_gather | solution.py:236
  711.5 13.3 convert_reduce_fusion
  726.8 6.4 convolution_convert_fusion.1
  733.2 75.4 %reduce-scatter.25.cloned.1.call-done = bf16[512,1024]{1,0:T(8,128)(2,1)} async-done(((bf16[2048,1024]{1,0:T(8,128)(2,1)}), bf16[512,1024]{1,0:T(8,128)(2,1)}) %reduce-scatter.25.cloned.1.call-update) | async-done | bytes 1048592 | tf_op jit(solution)/shard_map/reduce_scatter | solution.py:246
  808.6 3.3 multiply_reduce_fusion.1
  818.3 78.8 %all-gather.21.cloned.1.call-done = bf16[2048,1024]{1,0:T(8,128)(2,1)} async-done(((bf16[512,1024]{1,0:T(8,128)(2,1)}), bf16[2048,1024]{1,0:T(8,128)(2,1)}) %all-gather.21.cloned.1.call-update) | async-done | bytes 4194320 | tf_op jit(solution)/shard_map/all_gather | solution.py:256
  897.1 4.4 fusion.36
  901.5 276.6 %while.62 = (s32[]{:T(128)}, bf16[4,2048,64]{1,2,0:T(8,128)(2,1)}, bf16[4,2048,64]{1,2,0:T(8,128)(2,1)}, bf16[4,2048,64]{1,2,0:T(8,128)(2,1)}, s32[4]{0:T(128)S(...) while((s32[]{:T(128)}, bf16[4,2048,64]{1,2,0:T(8,128)(2,1)}, ...), condition=%wide.region_21.22_spmd, body=%wide.region_17.21_spmd.sunk | while | flops 682262016 | bytes 74622856 | solution.py:128
  912.9 54.7 %while.63 = (s32[]{:T(128)}, f32[2048,64]{0,1:T(8,128)}, f32[2048,64]{0,1:T(8,128)S(1)}, bf16[4,512,64]{1,2,0:T(8,128)(2,1)S(1)}, s32[4]{0:T(128)S(1)}, /*index=...) while((s32[]{:T(128)}, f32[2048,64]{0,1:T(8,128)}, ...), condition=%wide.region_20.20_spmd.clone, body=%wide.region_18.19_spmd.clone.sunk | while | flops 682262016 | bytes 68837712 | solution.py:123
  934.3 2.6 fusion.126
  948.0 2.6 fusion.126
  961.7 2.6 fusion.126
  982.0 54.7 %while.63 = (s32[]{:T(128)}, f32[2048,64]{0,1:T(8,128)}, f32[2048,64]{0,1:T(8,128)S(1)}, bf16[4,512,64]{1,2,0:T(8,128)(2,1)S(1)}, s32[4]{0:T(128)S(1)}, /*index=...) while((s32[]{:T(128)}, f32[2048,64]{0,1:T(8,128)}, ...), condition=%wide.region_20.20_spmd.clone, body=%wide.region_18.19_spmd.clone.sunk | while | flops 682262016 | bytes 68837712 | solution.py:123
  1003.4 2.6 fusion.126
  1051.2 54.7 %while.63 = (s32[]{:T(128)}, f32[2048,64]{0,1:T(8,128)}, f32[2048,64]{0,1:T(8,128)S(1)}, bf16[4,512,64]{1,2,0:T(8,128)(2,1)S(1)}, s32[4]{0:T(128)S(1)}, /*index=...) while((s32[]{:T(128)}, f32[2048,64]{0,1:T(8,128)}, ...), condition=%wide.region_20.20_spmd.clone, body=%wide.region_18.19_spmd.clone.sunk | while | flops 682262016 | bytes 68837712 | solution.py:123
  1120.3 54.7 %while.63 = (s32[]{:T(128)}, f32[2048,64]{0,1:T(8,128)}, f32[2048,64]{0,1:T(8,128)S(1)}, bf16[4,512,64]{1,2,0:T(8,128)(2,1)S(1)}, s32[4]{0:T(128)S(1)}, /*index=...) while((s32[]{:T(128)}, f32[2048,64]{0,1:T(8,128)}, ...), condition=%wide.region_20.20_spmd.clone, body=%wide.region_18.19_spmd.clone.sunk | while | flops 682262016 | bytes 68837712 | solution.py:123
  1141.7 2.6 fusion.126
  1181.4 16.9 %all-reduce.1 = (bf16[2,1024]{1,0:T(2,128)(2,1)S(1)}, bf16[2,1024]{1,0:T(2,128)(2,1)S(1)}, bf16[4096]{0:T(1024)(128)(2,1)S(1)}, bf16[2,1024]{1,0:T(2,128)(2,1)S(1)}, bf16[2,1024]{1,0:T(2,128)(2,1)S(1)}) all-reduce(bf16[2,1024]{1,0:T(2,128)(2,1)S(1)} %pad_maximum_fusion.1, ...), channel_id=1, replica_groups=mesh['dp'=8,'tensor'=4] {'tensor'}, use_global_device_ids=true, to_apply=%region_29.30 | all-reduce | flops 12288 | bytes 49152 | tf_op jit(solution)/shard_map/psum | solution.py:301
  1202.5 3.6 convolution_bitcast_fusion
  1214.8 3.4 add_convert_fusion
  1218.2 10.0 fusion.62
  1228.5 10.0 fusion.61
  1239.7 4.5 fusion.60
  1245.5 22.5 %all-reduce = f32[4096]{0:T(1024)S(1)} all-reduce(bf16[4096]{0:T(1024)(128)(2,1)S(1)} %get-tuple-element.521), channel_id=12, replica_groups=mesh['dp'=8,'tensor'=4] {'dp'}, use_global_device_ids=true, to_apply=%region_37.38.clone | all-reduce | flops 4096 | bytes 24576
  1271.7 35.6 %reduce-scatter.41.cloned.1.call-done = f32[128,2]{1,0:T(8,128)} async-done(((f32[1024,2]{1,0:T(8,128)}), f32[128,2]{1,0:T(8,128)}) %reduce-scatter.41.cloned.1.call-update) | async-done | bytes 1040
  1308.8 35.6 %reduce-scatter.43.cloned.1.call-done = f32[128,2]{1,0:T(8,128)} async-done(((f32[1024,2]{1,0:T(8,128)}), f32[128,2]{1,0:T(8,128)}) %reduce-scatter.43.cloned.1.call-update) | async-done | bytes 1040
  1345.8 48.4 %reduce-scatter.29.cloned.1.call-done = f32[3,128,256]{1,2,0:T(8,128)} async-done(((f32[3,1024,256]{1,2,0:T(8,128)}), f32[3,128,256]{1,2,0:T(8,128)}) %reduce-scatter.29.cloned.1.call-update) | async-done | bytes 393232 | tf_op jit(solution)/shard_map/reduce_scatter | solution.py:308
  1396.2 77.0 %reduce-scatter.27.cloned.1.call-done = bf16[512,1024]{1,0:T(8,128)(2,1)} async-done(((bf16[2048,1024]{1,0:T(8,128)(2,1)}), bf16[512,1024]{1,0:T(8,128)(2,1)}) %reduce-scatter.27.cloned.1.call-update) | async-done | bytes 1048592 | tf_op jit(solution)/shard_map/reduce_scatter | solution.py:279
  1475.7 53.5 %reduce-scatter.35.cloned.1.call-done = f32[128,1024]{1,0:T(8,128)} async-done(((f32[1024,1024]{1,0:T(8,128)}), f32[128,1024]{1,0:T(8,128)}) %reduce-scatter.35.cloned.1.call-update) | async-done | bytes 524304 | tf_op jit(solution)/shard_map/reduce_scatter | solution.py:243
  1529.2 55.1 %reduce-scatter.33.cloned.1.call-done = f32[128,1024]{1,0:T(8,128)} async-done(((f32[1024,1024]{1,0:T(8,128)}), f32[128,1024]{1,0:T(8,128)}) %reduce-scatter.33.cloned.1.call-update) | async-done | bytes 524304 | tf_op jit(solution)/shard_map/reduce_scatter | solution.py:242
  1584.3 40.1 %reduce-scatter.31.cloned.1.call-done = f32[128,256]{1,0:T(8,128)} async-done(((f32[1024,256]{1,0:T(8,128)}), f32[128,256]{1,0:T(8,128)}) %reduce-scatter.31.cloned.1.call-update) | async-done | bytes 131088 | tf_op jit(solution)/shard_map/reduce_scatter | solution.py:309
  (570 shorter events, 356.4 us)
Async XLA Ops:
  7.2 31.7 %all-gather.11.cloned.1.call-start = ((), (), s32[]{:S(2)}) async-start(), calls=%async_computation.13 | async-start | bytes 1769472 | tf_op jit(solution)/shard_map/all_gather | solution.py:166
  7.9 113.3 %all-gather.9.cloned.1.call-start = ((), (), s32[]{:S(2)}) async-start(), calls=%async_computation.12 | async-start | bytes 5242880 | tf_op jit(solution)/shard_map/all_gather | solution.py:189
  8.7 385.7 %reduce-scatter.21.cloned.1.call-start = ((), (), s32[]{:S(2)}) async-start(), calls=%async_computation.14 | async-start | bytes 5242880 | tf_op jit(solution)/shard_map/reduce_scatter | solution.py:203
  30.2 284.4 %copy-start.15 = (bf16[1024,256]{1,0:T(8,128)(2,1)}, bf16[1024,256]{1,0:T(8,128)(2,1)S(1)}, u32[]{:S(2)}) copy-start(bf16[1024,256]{1,0:T(8,128)(2,1)S(1)} %all_gather.46) | copy-start | bytes 1572868
  38.8 87.1 %copy-start.18 = (bf16[3,1024,256]{2,1,0:T(8,128)(2,1)S(1)}, bf16[3,1024,256]{2,1,0:T(8,128)(2,1)}, u32[]{:S(2)}) copy-start(bf16[3,1024,256]{2,1,0:T(8,128)(2,1)} %all-gather.11.cloned.1.call-done) | copy-start | bytes 4718596
  121.2 4.7 copy-start.30
  318.8 9.4 copy-start.28
  318.8 18.1 %copy-start.29 = (bf16[2,128]{1,0:T(2,128)(2,1)S(1)}, bf16[2,128]{1,0:T(2,128)(2,1)}, u32[]{:S(2)}) copy-start(bf16[2,128]{1,0:T(2,128)(2,1)} %param.27) | copy-start | bytes 1540
  318.8 75.5 %copy-start.3 = (bf16[512,1024]{1,0:T(8,128)(2,1)S(1)}, bf16[512,1024]{1,0:T(8,128)(2,1)}, u32[]{:S(2)}) copy-start(bf16[512,1024]{1,0:T(8,128)(2,1)} %param.18) | copy-start | bytes 3145732
  318.9 105.8 %all-gather.15.cloned.1.call-start = ((), (), s32[]{:S(2)}) async-start(), calls=%async_computation.16 | async-start | bytes 2359296 | tf_op jit(solution)/shard_map/all_gather | solution.py:168
  319.5 188.1 %all-gather.13.cloned.1.call-start = ((), (), s32[]{:S(2)}) async-start(), calls=%async_computation.15 | async-start | bytes 5242880 | tf_op jit(solution)/shard_map/all_gather | solution.py:214
  394.3 3.5 copy-start.4
  394.3 5.8 copy-start.26
  399.5 136.4 %all-gather.17.cloned.1.call-start = ((), (), s32[]{:S(2)}) async-start(), calls=%async_computation.17 | async-start | bytes 2359296 | tf_op jit(solution)/shard_map/all_gather | solution.py:169
  400.1 222.2 %reduce-scatter.23.cloned.1.call-start = ((), (), s32[]{:S(2)}) async-start(), calls=%async_computation.18 | async-start | bytes 5242880 | tf_op jit(solution)/shard_map/reduce_scatter | solution.py:219
  545.3 79.5 %copy-start.9 = (bf16[512,1024]{1,0:T(8,128)(2,1)S(1)}, bf16[512,1024]{1,0:T(8,128)(2,1)}, u32[]{:S(2)}) copy-start(bf16[512,1024]{1,0:T(8,128)(2,1)} %param.29) | copy-start | bytes 3145732
  545.3 166.2 %all-gather.19.cloned.1.call-start = ((), (), s32[]{:S(2)}) async-start(), calls=%async_computation.19 | async-start | bytes 5242880 | tf_op jit(solution)/shard_map/all_gather | solution.py:236
  630.1 178.6 %reduce-scatter.25.cloned.1.call-start = ((), (), s32[]{:S(2)}) async-start(), calls=%async_computation.20 | async-start | bytes 5242880 | tf_op jit(solution)/shard_map/reduce_scatter | solution.py:246
  711.5 15.3 copy-start.32
  733.2 163.9 %all-gather.21.cloned.1.call-start = ((), (), s32[]{:S(2)}) async-start(), calls=%async_computation.21 | async-start | bytes 5242880 | tf_op jit(solution)/shard_map/all_gather | solution.py:256
  808.6 3.3 copy-start.6
  808.6 3.3 copy-start.14
  813.1 84.0 %copy-start.16 = (bf16[1024,256]{1,0:T(8,128)(2,1)S(1)}, bf16[1024,256]{1,0:T(8,128)(2,1)}, u32[]{:S(2)}) copy-start(bf16[1024,256]{1,0:T(8,128)(2,1)} %copy-done.15) | copy-start | bytes 1572868
  813.1 88.4 %copy-start.21 = (f32[512]{0:T(512)}, f32[512]{0:T(512)S(1)}, u32[]{:S(2)}) copy-start(f32[512]{0:T(512)S(1)} %negate_multiply_fusion.1) | copy-start | bytes 6148
  815.7 453.1 %reduce-scatter.37.cloned.1.call-start = ((), (), s32[]{:S(2)}) async-start(), calls=%async_computation.27 | async-start | bytes 589824
  816.4 85.1 %copy-start.20 = (bf16[4096]{0:T(1024)(128)(2,1)}, bf16[4096]{0:T(1024)(128)(2,1)S(1)}, u32[]{:S(2)}) copy-start(bf16[4096]{0:T(1024)(128)(2,1)S(1)} %dynamic_update_slice.50) | copy-start | bytes 24580
  901.5 279.9 %copy-start.23 = (bf16[2,1024]{1,0:T(2,128)(2,1)S(1)}, bf16[2,1024]{1,0:T(2,128)(2,1)}, u32[]{:S(2)}) copy-start(bf16[2,1024]{1,0:T(2,128)(2,1)} %pad_maximum_fusion.2) | copy-start | bytes 12292
  901.5 279.9 %copy-start.24 = (bf16[2,1024]{1,0:T(2,128)(2,1)S(1)}, bf16[2,1024]{1,0:T(2,128)(2,1)}, u32[]{:S(2)}) copy-start(bf16[2,1024]{1,0:T(2,128)(2,1)} %pad_maximum_fusion.3) | copy-start | bytes 12292
  901.5 279.9 %copy-start.25 = (bf16[2,1024]{1,0:T(2,128)(2,1)S(1)}, bf16[2,1024]{1,0:T(2,128)(2,1)}, u32[]{:S(2)}) copy-start(bf16[2,1024]{1,0:T(2,128)(2,1)} %pad_maximum_fusion.4) | copy-start | bytes 12292
  918.3 2.0 copy-start
  920.7 4.2 copy-start.1
  934.3 4.4 copy-start.1
  948.0 4.4 copy-start.1
  961.7 4.4 copy-start.1
  989.9 4.2 copy-start.1
  1003.4 4.4 copy-start.1
  1014.7 2.0 copy-start
  1017.1 4.4 copy-start.1
  1030.9 4.4 copy-start.1
  1056.7 2.0 copy-start
  1059.1 4.2 copy-start.1
  1072.6 4.4 copy-start.1
  1086.3 4.4 copy-start.1
  1100.0 4.4 copy-start.1
  1125.8 2.0 copy-start
  1128.2 4.2 copy-start.1
  1141.7 4.4 copy-start.1
  1155.5 4.4 copy-start.1
  1169.2 4.4 copy-start.1
  1178.2 24.4 %copy-start.13 = (bf16[4,2048,64]{1,2,0:T(8,128)(2,1)S(1)}, bf16[4,2048,64]{1,2,0:T(8,128)(2,1)}, u32[]{:S(2)}) copy-start(bf16[4,2048,64]{1,2,0:T(8,128)(2,1)} %get-tuple-element.324) | copy-start | bytes 3145732
  1199.3 70.9 %reduce-scatter.39.cloned.1.call-start = ((), (), s32[]{:S(2)}) async-start(), calls=%async_computation.28 | async-start | bytes 589824
  1200.3 107.0 %reduce-scatter.41.cloned.1.call-start = ((), (), s32[]{:S(2)}) async-start(), calls=%async_computation.29 | async-start | bytes 589824
  1201.4 143.0 %reduce-scatter.43.cloned.1.call-start = ((), (), s32[]{:S(2)}) async-start(), calls=%async_computation.30 | async-start | bytes 589824
  1201.4 4.7 copy-start.17
  1202.5 191.8 %reduce-scatter.29.cloned.1.call-start = ((), (), s32[]{:S(2)}) async-start(), calls=%async_computation.23 | async-start | bytes 3538944 | tf_op jit(solution)/shard_map/reduce_scatter | solution.py:308
  1202.5 3.7 copy-start.31
  1210.7 262.5 %reduce-scatter.27.cloned.1.call-start = ((), (), s32[]{:S(2)}) async-start(), calls=%async_computation.22 | async-start | bytes 5242880 | tf_op jit(solution)/shard_map/reduce_scatter | solution.py:279
  1211.0 2.5 copy-start.19
  1218.2 311.0 %reduce-scatter.35.cloned.1.call-start = ((), (), s32[]{:S(2)}) async-start(), calls=%async_computation.26 | async-start | bytes 4718592 | tf_op jit(solution)/shard_map/reduce_scatter | solution.py:243
  1228.2 356.1 %reduce-scatter.33.cloned.1.call-start = ((), (), s32[]{:S(2)}) async-start(), calls=%async_computation.25 | async-start | bytes 4718592 | tf_op jit(solution)/shard_map/reduce_scatter | solution.py:242
  1238.5 5.8 copy-start.33
  1238.5 234.7 %copy-start.8 = (f32[512,1024]{1,0:T(8,128)S(1)}, f32[512,1024]{1,0:T(8,128)}, u32[]{:S(2)}) copy-start(f32[512,1024]{1,0:T(8,128)} %copy-done.7) | copy-start | bytes 6291460
  1238.6 234.6 %copy-start.22 = (f32[512]{0:T(512)S(1)}, f32[512]{0:T(512)}, u32[]{:S(2)}) copy-start(f32[512]{0:T(512)} %copy-done.21) | copy-start | bytes 6148
  1238.6 385.9 %reduce-scatter.31.cloned.1.call-start = ((), (), s32[]{:S(2)}) async-start(), calls=%async_computation.24 | async-start | bytes 1179648 | tf_op jit(solution)/shard_map/reduce_scatter | solution.py:309
  (35 other events, 63.3 us)
Sparse Core Ops, SparseCore 0:
  9.9 28.8 all-gather.10
  40.4 80.7 all-gather.8
  319.0 75.2 reduce-scatter.20
  396.2 28.4 all-gather.14
  426.8 80.7 all-gather.12
  509.5 26.4 all-gather.16
  545.4 76.7 reduce-scatter.22
  630.2 81.2 all-gather.18
  733.3 75.2 reduce-scatter.24
  815.8 81.2 all-gather.20
  1199.4 33.1 reduce-scatter.36
  1235.6 34.1 reduce-scatter.38
  1273.1 34.1 reduce-scatter.40
  1310.2 34.0 reduce-scatter.42
  1348.0 46.2 reduce-scatter.28
  1396.4 76.7 reduce-scatter.26
  1477.3 51.7 reduce-scatter.34
  1533.0 51.3 reduce-scatter.32
  1588.4 35.9 reduce-scatter.30
where the time goes:
time: 1640 us; the launch traced here: 1630 us
  waiting for transfers between devices  901 us (55%)
  matrix products  355 us (22%)
  local copies, waits for them, and re-layouts  119 us (7%)
  loops' own time  99.2 us (6%)
  blocking collectives  94.2 us (6%)
  other arithmetic  45.7 us (3%)
    dot_general x38, matrix products, matmul(): return jnp.dot(left, right, preferred_element_type=jnp.float32)  136 us
    dot_general x54, matrix products, matmul_nt(): lax.dot_general(left, right, (((1,), (1,)), ((), ())), preferred_element_...  124 us
    dot_general x38, matrix products, matmul_tn(): lax.dot_general(left, right, (((0,), (0,)), ((), ())), preferred_element_...  94.7 us
    all_gather x1, waiting for transfers between devices, on_device(): lax.all_gather(normed_one.astype(jnp.bfloat16), 'tensor', axis=0, tiled=T...  82.9 us
    all_gather x1, waiting for transfers between devices, on_device(): inputs = lax.all_gather(tokens, 'tensor', axis=0, tiled=True)  82.4 us
    all_gather x1, waiting for transfers between devices, on_device(): grad_mixed_all = lax.all_gather(grad_mixed, 'tensor', axis=0, tiled=True)  81.4 us
    all_gather x1, waiting for transfers between devices, on_device(): grad_att_all = lax.all_gather(grad_attended, 'tensor', axis=0, tiled=True)  78.8 us
    reduce_scatter x1, waiting for transfers between devices, on_device(): lax.psum_scatter((total + matmul_nt(grad_values, qkv_all[2])).astype(jnp....  77 us
  transfers between devices with their start and end apart: 19, of which 17 were waited for; matrix products, arithmetic and copies ran while one was open for 5% of the time, Pallas kernels for 0%

commit v1 on v0

v1 whole, which is shorter than its diff:
```python
import functools

import jax
import jax.numpy as jnp
from jax import lax
from jax.experimental import pallas as pl
from jax.experimental.pallas import tpu as pltpu
from jax.sharding import PartitionSpec as P

HD = 64
LEN = 2048


epsilon = 1e-06


def layer_norm(rows, gain, shift):
    centred = rows - jnp.mean(rows, -1, keepdims=True)
    spread = jnp.mean(centred * centred, -1, keepdims=True)
    return centred * lax.rsqrt(spread + epsilon) * gain + shift


def gelu_exact(values):
    return jax.nn.gelu(values, approximate=False)


def segment_ids(lengths, length):
    ends = jnp.cumsum(lengths, axis=-1)
    places = jnp.arange(length, dtype=jnp.int32)
    return jnp.sum((places[None, :, None] >= ends[:, None, :]).astype(jnp.int32), -1)


def matmul(left, right):
    return jnp.dot(left, right, preferred_element_type=jnp.float32)


def matmul_nt(left, right):
    return lax.dot_general(
        left, right, (((1,), (1,)), ((), ())), preferred_element_type=jnp.float32
    )


def matmul_tn(left, right):
    return lax.dot_general(
        left, right, (((0,), (0,)), ((), ())), preferred_element_type=jnp.float32
    )


def forward_kernel(heads, head_dim, block, ranges, q_t, k, v_t, seg_q, seg_k, ctx_t, lse):
    index = pl.program_id(0)
    low, high = ranges[0, index], ranges[1, index]
    local = heads * head_dim
    query = q_t[...]
    rows = lax.broadcasted_iota(jnp.int32, (local, block), 0) // head_dim
    masked = [jnp.where(rows == h, query, jnp.zeros_like(query)) for h in range(heads)]
    seg_row = seg_q[0:1, :]

    def step(j, carry):
        at = pl.ds(pl.multiple_of(j * block, block), block)
        keys = k[at, :]
        same = seg_k[at, :] == seg_row
        new = []
        for h in range(heads):
            peak, total, acc = carry[h]
            scores = jnp.dot(keys, masked[h], preferred_element_type=jnp.float32)
            scores = jnp.where(same, scores, -1e30)
            top = jnp.maximum(peak, jnp.max(scores, 0, keepdims=True))
            powered = jnp.exp(scores - top)
            shrink = jnp.exp(peak - top)
            total = total * shrink + jnp.sum(powered, 0, keepdims=True)
            part = jnp.dot(
                v_t[h * head_dim : (h + 1) * head_dim, at],
                powered.astype(jnp.bfloat16),
                preferred_element_type=jnp.float32,
            )
            new.append((top, total, acc * shrink + part))
        return tuple(new)

    first = tuple(
        (
            jnp.full((1, block), -1e30, jnp.float32),
            jnp.zeros((1, block), jnp.float32),
            jnp.zeros((head_dim, block), jnp.float32),
        )
        for _ in range(heads)
    )
    done = lax.fori_loop(low, high, step, first)
    for h in range(heads):
        peak, total, acc = done[h]
        ctx_t[h * head_dim : (h + 1) * head_dim, :] = acc / total
        lse[h : h + 1, :] = peak + jnp.log(total)


def backward_kernel(
    heads, head_dim, block, ranges, q_t, q, k, k_t, v, g_t, g, ctx_t, lse, seg_q, seg_k,
    dq_t, dk, dv, dk_sum, dv_sum,
):
    index = pl.program_id(0)
    low, high = ranges[0, index], ranges[1, index]
    local = heads * head_dim

    @pl.when(index == 0)
    def _():
        dk_sum[...] = jnp.zeros_like(dk_sum)
        dv_sum[...] = jnp.zeros_like(dv_sum)

    rows = lax.broadcasted_iota(jnp.int32, (local, block), 0) // head_dim
    lanes = lax.broadcasted_iota(jnp.int32, (block, local), 1) // head_dim
    query_t, query, grad_t, grad = q_t[...], q[...], g_t[...], g[...]
    zero_t, zero = jnp.zeros_like(query_t), jnp.zeros_like(query)
    products = grad_t.astype(jnp.float32) * ctx_t[...]
    inner = [
        jnp.sum(products[h * head_dim : (h + 1) * head_dim, :], 0, keepdims=True)
        for h in range(heads)
    ]
    qs_t = [jnp.where(rows == h, query_t, zero_t) for h in range(heads)]
    gs_t = [jnp.where(rows == h, grad_t, zero_t) for h in range(heads)]
    qs = [jnp.where(lanes == h, query, zero) for h in range(heads)]
    gs = [jnp.where(lanes == h, grad, zero) for h in range(heads)]
    seg_row = seg_q[0:1, :]

    def step(j, carry):
        at = pl.ds(pl.multiple_of(j * block, block), block)
        keys, vals = k[at, :], v[at, :]
        same = seg_k[at, :] == seg_row
        new = []
        d_keys = jnp.zeros((block, local), jnp.float32)
        d_vals = jnp.zeros((block, local), jnp.float32)
        for h in range(heads):
            scores = jnp.dot(keys, qs_t[h], preferred_element_type=jnp.float32)
            weights = jnp.exp(jnp.where(same, scores - lse[h : h + 1, :], -1e30))
            d_weights = jnp.dot(vals, gs_t[h], preferred_element_type=jnp.float32)
            d_scores = (weights * (d_weights - inner[h])).astype(jnp.bfloat16)
            d_vals += jnp.dot(
                weights.astype(jnp.bfloat16), gs[h], preferred_element_type=jnp.float32
            )
            d_keys += jnp.dot(d_scores, qs[h], preferred_element_type=jnp.float32)
            new.append(
                carry[h]
                + jnp.dot(
                    k_t[h * head_dim : (h + 1) * head_dim, at],
                    d_scores,
                    preferred_element_type=jnp.float32,
                )
            )
        dk_sum[at, :] += d_keys
        dv_sum[at, :] += d_vals
        return tuple(new)

    first = tuple(jnp.zeros((head_dim, block), jnp.float32) for _ in range(heads))
    done = lax.fori_loop(low, high, step, first)
    for h in range(heads):
        dq_t[h * head_dim : (h + 1) * head_dim, :] = (done[h] * head_dim**-0.5).astype(
            jnp.bfloat16
        )

    @pl.when(index == pl.num_programs(0) - 1)
    def _():
        dk[...] = dk_sum[...].astype(jnp.bfloat16)
        dv[...] = dv_sum[...].astype(jnp.bfloat16)


def whole(shape):
    return pl.BlockSpec(shape, lambda i: (0, 0))


def attend_forward(ranges, q_t, k, v_t, seg_q, seg_k, head_dim, block):
    local, length = q_t.shape
    heads = local // head_dim
    cols = pl.BlockSpec((local, block), lambda i: (0, i))
    few = pl.BlockSpec((8, block), lambda i: (0, i))
    return pl.pallas_call(
        functools.partial(forward_kernel, heads, head_dim, block),
        grid=(length // block,),
        in_specs=[
            pl.BlockSpec(memory_space=pltpu.SMEM),
            cols,
            whole((length, local)),
            whole((local, length)),
            few,
            whole((length, 1)),
        ],
        out_specs=[cols, few],
        out_shape=[
            jax.ShapeDtypeStruct((local, length), jnp.float32),
            jax.ShapeDtypeStruct((8, length), jnp.float32),
        ],
        compiler_params=pltpu.CompilerParams(vmem_limit_bytes=48 * 2**20),
        cost_estimate=pl.CostEstimate(
            flops=16 * length * length * local,
            bytes_accessed=8 * length * local,
            transcendentals=heads * length * length,
        ),
    )(ranges, q_t, k, v_t, seg_q, seg_k)


def attend_backward(ranges, q_t, q, k, k_t, v, g_t, g, ctx_t, lse, seg_q, seg_k, head_dim, block):
    local, length = q_t.shape
    heads = local // head_dim
    cols = pl.BlockSpec((local, block), lambda i: (0, i))
    rows = pl.BlockSpec((block, local), lambda i: (i, 0))
    few = pl.BlockSpec((8, block), lambda i: (0, i))
    tall, wide = whole((length, local)), whole((local, length))
    return pl.pallas_call(
        functools.partial(backward_kernel, heads, head_dim, block),
        grid=(length // block,),
        in_specs=[
            pl.BlockSpec(memory_space=pltpu.SMEM),
            cols, rows, tall, wide, tall, cols, rows, cols, few, few,
            whole((length, 1)),
        ],
        out_specs=[cols, tall, tall],
        out_shape=[
            jax.ShapeDtypeStruct((local, length), jnp.bfloat16),
            jax.ShapeDtypeStruct((length, local), jnp.bfloat16),
            jax.ShapeDtypeStruct((length, local), jnp.bfloat16),
        ],
        scratch_shapes=[
            pltpu.VMEM((length, local), jnp.float32),
            pltpu.VMEM((length, local), jnp.float32),
        ],
        compiler_params=pltpu.CompilerParams(vmem_limit_bytes=48 * 2**20),
        cost_estimate=pl.CostEstimate(
            flops=40 * length * length * local,
            bytes_accessed=16 * length * local,
            transcendentals=heads * length * length,
        ),
    )(ranges, q_t, q, k, k_t, v, g_t, g, ctx_t, lse, seg_q, seg_k)


def column_sum(array):
    return jnp.sum(array.astype(jnp.float32), 0)


def dot(left, right, left_at, right_at):
    return lax.dot_general(
        left, right, (((left_at,), (right_at,)), ((), ())), preferred_element_type=jnp.float32
    )


def on_device(
    tokens,
    w_qkv,
    w_attn_out,
    w_in,
    w_out,
    b_qv,
    b_proj,
    b_hidden,
    ln_gain,
    ln_bias,
    doc_lengths,
    cotangent,
):
    head_dim = HD
    low = jnp.bfloat16
    rows_here, width = tokens.shape
    members = lax.axis_size("tensor")
    groups = lax.axis_size("dp")
    position = lax.axis_index("tensor")
    place = lax.axis_index("dp")
    part, local = w_qkv.shape[1:]
    hidden_all = w_in.shape[1] * members
    block = 256

    vectors = jnp.concatenate(
        [a.reshape(-1) for a in (b_qv, b_proj, ln_gain, ln_bias, b_hidden)]
    )
    inputs = lax.all_gather(tokens, "tensor", axis=0, tiled=True)
    lead = -(-vectors.size // local)
    lead += -lead % 16
    packed = jnp.concatenate(
        [
            w_qkv.reshape(3 * part, local),
            jnp.pad(vectors, (0, lead * local - vectors.size)).reshape(lead, local),
        ]
    )
    packed = lax.all_gather(packed, "dp", axis=0, tiled=False)
    qkv_all = (
        packed[:, : 3 * part]
        .reshape(groups, 3, part, local)
        .transpose(1, 0, 2, 3)
        .reshape(3, width, local)
    )
    vectors = packed[:, 3 * part :].reshape(groups, lead * local)

    def pairs(index):
        pieces = vectors[:, 2 * part * index : 2 * part * (index + 1)]
        pieces = pieces.reshape(groups, 2, part).transpose(1, 0, 2)
        return pieces.reshape(2, width).astype(jnp.float32)

    qv_bias, proj_bias, gains, shifts = (pairs(index) for index in range(4))
    hidden_bias = vectors[:, 8 * part : 8 * part + b_hidden.size].reshape(-1).astype(jnp.float32)
    query_bias = lax.dynamic_slice_in_dim(qv_bias[0], position * local, local)
    value_bias = lax.dynamic_slice_in_dim(qv_bias[1], position * local, local)

    def everywhere(w):
        w = lax.all_gather(w, "tensor", axis=1, tiled=True)
        return lax.all_gather(w, "dp", axis=0, tiled=True)

    attn_out_all, in_all, out_all = everywhere(w_attn_out), everywhere(w_in), everywhere(w_out)

    segments = segment_ids(doc_lengths, LEN)[0]
    seg_k = segments[:, None]
    seg_q = jnp.broadcast_to(segments[None, :], (8, LEN))
    ends = jnp.cumsum(doc_lengths[0])
    starts = jnp.arange(LEN // block, dtype=jnp.int32)[:, None] * block
    lows = jnp.max(jnp.where(ends[None, :] <= starts, ends[None, :], 0), -1)
    highs = jnp.min(jnp.where(ends[None, :] >= starts + block, ends[None, :], LEN), -1)
    ranges = jnp.stack([lows // block, (highs + block - 1) // block]).astype(jnp.int32)

    queries = (matmul(inputs, qkv_all[0]) + query_bias).astype(low) * jnp.asarray(
        head_dim**-0.5, low
    )
    keys = matmul(inputs, qkv_all[1]).astype(low)
    values = (matmul(inputs, qkv_all[2]) + value_bias).astype(low)
    queries_t, keys_t, values_t = queries.T, keys.T, values.T
    context_t, log_sums = attend_forward(
        ranges, queries_t, keys, values_t, seg_q, seg_k, head_dim, block
    )
    context = lax.all_to_all(
        context_t.T.astype(low).reshape(members, rows_here, local),
        "tensor", split_axis=0, concat_axis=0, tiled=False,
    )
    context = context.transpose(1, 0, 2).reshape(rows_here, width)
    attended = matmul_nt(context, attn_out_all) + proj_bias[0]
    normed_one, norm_one_pull = jax.vjp(
        layer_norm, tokens.astype(jnp.float32) + attended, gains[0], shifts[0]
    )
    normed = normed_one.astype(low)
    hidden_pre = matmul(normed, in_all) + hidden_bias
    activated, gelu_pull = jax.vjp(gelu_exact, hidden_pre)
    activated = activated.astype(low)
    mixed = matmul_nt(activated, out_all) + proj_bias[1]
    output, norm_two_pull = jax.vjp(layer_norm, normed_one + mixed, gains[1], shifts[1])
    grad_two, gain_two, shift_two = norm_two_pull(cotangent.astype(jnp.float32))
    grad_mixed = grad_two.astype(low)
    grad_pre = gelu_pull(matmul(grad_mixed, out_all))[0].astype(low)
    grad_normed = matmul_nt(grad_pre, in_all) + grad_two
    grad_one, gain_one, shift_one = norm_one_pull(grad_normed)
    grad_attended = grad_one.astype(low)
    grad_context = matmul(grad_attended, attn_out_all).astype(low)
    grad_context = lax.all_to_all(
        grad_context.reshape(rows_here, members, local).transpose(1, 0, 2),
        "tensor", split_axis=0, concat_axis=0, tiled=False,
    ).reshape(rows_here * members, local)

    def owned(grad):
        grad = lax.psum_scatter(grad.astype(low), "dp", scatter_dimension=0, tiled=True)
        grad = lax.psum_scatter(grad, "tensor", scatter_dimension=1, tiled=True)
        return grad.astype(jnp.float32)

    grad_in = owned(matmul_tn(normed, grad_pre))
    grad_out = owned(matmul_tn(grad_mixed, activated))
    grad_attn_out = owned(matmul_tn(grad_attended, context))

    grad_queries_t, grad_keys, grad_values = attend_backward(
        ranges, queries_t, queries, keys, keys_t, values, grad_context.T, grad_context,
        context_t, log_sums, seg_q, seg_k, head_dim, block,
    )
    total = dot(grad_queries_t, qkv_all[0], 0, 1)
    total = total + matmul_nt(grad_keys, qkv_all[1])
    total = total + matmul_nt(grad_values, qkv_all[2])
    grad_tokens = (
        lax.psum_scatter(
            total.astype(low), "tensor", scatter_dimension=0, tiled=True
        ).astype(jnp.float32)
        + grad_one
    ).astype(low)
    grad_qkv = jnp.stack(
        [
            dot(inputs, grad_queries_t, 0, 1),
            matmul_tn(inputs, grad_keys),
            matmul_tn(inputs, grad_values),
        ]
    ).astype(low)
    grad_qkv = lax.psum_scatter(grad_qkv, "dp", scatter_dimension=1, tiled=True)
    grad_qkv = grad_qkv.astype(jnp.float32)

    def placed(piece):
        return lax.dynamic_update_slice_in_dim(
            jnp.zeros((width,), jnp.float32), piece, position * local, 0
        )

    sums = jnp.concatenate(
        [
            jnp.stack(
                [
                    placed(jnp.sum(grad_queries_t.astype(jnp.float32), 1)),
                    placed(column_sum(grad_values)),
                    column_sum(grad_attended),
                    column_sum(grad_mixed),
                    gain_one,
                    gain_two,
                    shift_one,
                    shift_two,
                ]
            ),
            column_sum(grad_pre).reshape(-1, width),
        ]
    )
    sums = lax.psum(sums, ("dp", "tensor"))
    pieces = lax.dynamic_slice_in_dim(sums[:8], place * part, part, 1)
    grad_hidden = lax.dynamic_slice_in_dim(
        sums[8:].reshape(-1), place * b_hidden.size, b_hidden.size, 0
    )
    return (
        output.astype(low),
        grad_tokens,
        grad_qkv,
        grad_attn_out,
        grad_in,
        grad_out,
        pieces[0:2],
        pieces[2:4],
        grad_hidden,
        pieces[4:6],
        pieces[6:8],
    )


def solution(mesh):
    in_specs = (
        P(("dp", "tensor"), None),
        P(None, "dp", "tensor"),
        P("dp", "tensor"),
        P("dp", "tensor"),
        P("dp", "tensor"),
        P(None, "dp"),
        P(None, "dp"),
        P("dp"),
        P(None, "dp"),
        P(None, "dp"),
        P("dp", None),
        P(("dp", "tensor"), None),
    )
    out_specs = (
        P(("dp", "tensor"), None),
        P(("dp", "tensor"), None),
        P(None, "dp", "tensor"),
        P("dp", "tensor"),
        P("dp", "tensor"),
        P("dp", "tensor"),
        P(None, "dp"),
        P(None, "dp"),
        P("dp"),
        P(None, "dp"),
        P(None, "dp"),
    )
    return jax.shard_map(
        on_device, mesh=mesh, in_specs=in_specs, out_specs=out_specs, check_vma=False
    )
```

time: 1640 us -> 785 us (0.48)
  waiting for transfers between devices: 901 us -> 364 us
  matrix products: 355 us -> 113 us
  Pallas kernels: 0 us -> 138 us
  loops' own time: 99.2 us -> 0 us
  local copies, waits for them, and re-layouts: 119 us -> 35.6 us
  other arithmetic: 45.7 us -> 19.5 us
    reduce_scatter x8 -> x7, waiting for transfers between devices: 475 us -> 175 us  [the longest x1 76.9 us: on_device(): lax.psum_scatter(total.astype(low), 'tensor', scatter_dimension=0, tiled=...]
    all_gather x6, waiting for transfers between devices: 270 us -> 64 us  [the longest x2 36 us: everywhere(): w = lax.all_gather(w, 'tensor', axis=1, tiled=True)]
    pallas_call x0 -> x2, Pallas kernels: none -> 138 us  [the longest x1 71.4 us: attend_forward(): pl.pallas_call(functools.partial(forward_kernel, heads, head_dim, block),...]
    dot_general x54 -> x5, matrix products: 124 us -> 23.9 us  [matmul_nt(): lax.dot_general(left, right, (((1,), (1,)), ((), ())), preferred_element_...]
    another operation x6 -> x0, loops' own time: 99.2 us -> none  [the longest x1 43.1 us: attend_forward(): lax.map(attend_one_block, jnp.arange(seqs * heads * blocks, dtype=jnp.int...]
    dot_general x38 -> x6, matrix products: 136 us -> 57.2 us  [matmul(): return jnp.dot(left, right, preferred_element_type=jnp.float32)]
    dot_general x38 -> x5, matrix products: 94.7 us -> 25.5 us  [matmul_tn(): lax.dot_general(left, right, (((0,), (0,)), ((), ())), preferred_element_...]
    unnamed x23 -> x16, waiting for transfers between devices: 73.9 us -> 21.5 us
  transfers between devices with their start and end apart: 19 -> 16, of which waited for: 17 -> 10; matrix products, arithmetic and copies ran while one was open for 5% -> 15% of each run, Pallas kernels for 0% -> 18%
where the time goes in v1:
time: 785 us; the launch traced here: 776 us
  waiting for transfers between devices  364 us (46%)
  Pallas kernels  138 us (18%)
  matrix products  113 us (14%)
  blocking collectives  86.4 us (11%)
  local copies, waits for them, and re-layouts  35.6 us (5%)
  other arithmetic  19.5 us (2%)
  between operations  14.7 us (2%)
    all_gather x1, waiting for transfers between devices, on_device(): inputs = lax.all_gather(tokens, 'tensor', axis=0, tiled=True)  78.7 us
    reduce_scatter x1, waiting for transfers between devices, on_device(): lax.psum_scatter(total.astype(low), 'tensor', scatter_dimension=0, tiled=...  76.9 us
    pallas_call x1, Pallas kernels, attend_forward(): pl.pallas_call(functools.partial(forward_kernel, heads, head_dim, block),...  71.4 us
    pallas_call x1, Pallas kernels, attend_backward(): pl.pallas_call(functools.partial(backward_kernel, heads, head_dim, block)...  66.5 us
    dot_general x6, matrix products, matmul(): return jnp.dot(left, right, preferred_element_type=jnp.float32)  57.2 us
    reduce_scatter x3, waiting for transfers between devices, owned(): grad = lax.psum_scatter(grad, 'tensor', scatter_dimension=1, tiled=True)  53.6 us
    reduce_scatter x3, waiting for transfers between devices, owned(): lax.psum_scatter(grad.astype(low), 'dp', scatter_dimension=0, tiled=True)  44.1 us
    psum x1, blocking collectives, on_device(): sums = lax.psum(sums, ('dp', 'tensor'))  39.7 us
  transfers between devices with their start and end apart: 16, of which 10 were waited for; matrix products, arithmetic and copies ran while one was open for 15% of the time, Pallas kernels for 18%

profile of v1, /device:TPU:0, one launch (start us, length us, event | category | flops | bytes accessed | tf_op | source)
XLA Modules:
  0.0 776.0 jit_solution(2876273561583723912)
XLA Ops:
  8.7 0.9 dynamic-update-slice
  9.6 0.8 dynamic-update-slice.1
  12.8 1.6 pad_maximum_fusion.1
  15.1 19.3 %all_gather.30 = bf16[128,1024]{1,0:T(8,128)(2,1)} all-gather(bf16[128,256]{1,0:T(8,128)(2,1)} %param.14), channel_id=1, replica_groups=mesh['dp'=8,'tensor'=4] {'tensor'}, dimensions={1}, use_global_device_ids=true | all-gather | bytes 327680 | tf_op jit(solution)/shard_map/all_gather | solution.py:298
  34.5 9.7 %all-gather.13.cloned.1.call-done = bf16[128,4096]{1,0:T(8,128)(2,1)} async-done(((bf16[128,1024]{1,0:T(8,128)(2,1)}), bf16[128,4096]{1,0:T(8,128)(2,1)}) %all-gather.13.cloned.1.call-update) | async-done | bytes 1048592 | tf_op jit(solution)/shard_map/all_gather | solution.py:298
  46.5 26.3 %all-gather.17.cloned.1.call-done = bf16[128,4096]{1,0:T(8,128)(2,1)} async-done(((bf16[128,1024]{1,0:T(8,128)(2,1)}), bf16[128,4096]{1,0:T(8,128)(2,1)}) %all-gather.17.cloned.1.call-update) | async-done | bytes 1048592 | tf_op jit(solution)/shard_map/all_gather | solution.py:298
  72.8 27.9 %all-gather.21.cloned.1.call-done = bf16[3200,256]{1,0:T(8,128)(2,1)} async-done(((bf16[400,256]{1,0:T(8,128)(2,1)}), bf16[3200,256]{1,0:T(8,128)(2,1)}) %all-gather.21.cloned.1.call-update) | async-done | bytes 1638416 | tf_op jit(solution)/shard_map/all_gather | solution.py:278
  100.8 0.8 slice_bitcast_fusion
  101.6 1.5 slice.116
  103.2 1.1 fusion.25
  104.3 78.7 %all-gather.9.cloned.1.call-done = bf16[2048,1024]{1,0:T(8,128)(2,1)} async-done(((bf16[512,1024]{1,0:T(8,128)(2,1)}), bf16[2048,1024]{1,0:T(8,128)(2,1)}) %all-gather.9.cloned.1.call-update) | async-done | bytes 4194320 | tf_op jit(solution)/shard_map/all_gather | solution.py:269
  183.0 3.5 fusion.10
  187.1 5.0 convolution_convert_fusion.2.k_t
  192.2 1.5 copy.62.k
  193.7 4.9 fusion.7
  198.6 2.3 copy.63.v_t
  200.9 1.3 copy-done.6
  202.2 71.4 %shard_map.203 = (f32[256,2048]{1,0:T(8,128)}, f32[8,2048]{1,0:T(8,128)S(1)}) custom-call(s32[2,8]{1,0:T(2,128)S(1)} %pad_add_fusion.ranges, bf16[256,2048]{1,0:T(8,128)(2,1)S(1)} %copy.61.q_t, bf16[2048,256]{1,0:T(8,128)(2,1)S(1)} %copy.62.k, bf16[256,2048]{1,0:T(8,128)(2,1)S(1)} %copy-done.6, s32[8,2048]{1,0:T(8,128)S(1)} %broadcast_in_dim.28.seg_q, ...), custom_call_target="tpu_custom_call" | custom-call | flops 17179869184 | bytes 4194304 | tf_op jit(solution)/shard_map/pallas_call | solution.py:172
  273.6 1.8 convert_element_type.166
  275.5 1.1 copy.86
  276.5 3.6 all-to-all-start
  280.4 25.6 %all-to-all-done = bf16[4,512,256]{1,2,0:T(8,128)(2,1)S(1)} async-done(((bf16[4,512,256]{1,2,0:T(8,128)(2,1)}), bf16[4,512,256]{1,2,0:T(8,128)(2,1)S(1)}, u32[]{:S(2)}, u32[]{:S(2)}) %all-to-all-start) | async-done | bytes 1048608 | tf_op jit(solution)/shard_map/all_to_all | solution.py:321
  305.9 1.0 copy-done.15
  306.9 3.3 fusion.28
  310.6 27.8 %multiply_convert_fusion = (bf16[512,4096]{1,0:T(8,128)(2,1)}, f32[512,4096]{1,0:T(8,128)}, f32[512,4096]{1,0:T(8,128)}) fusion(f32[4096]{0:T(1024)S(1)} %bitcast.198, bf16[1024,4096]{1,0:T(8,128)(2,1)} %all-gather.15.cloned.1.call-done, f32[512,1024]{1,0:T(8,128)S(1)} %get-tuple-element.106, f32[1024]{0:T(1024)S(1)} %get-tuple-element.96, ...), kind=kOutput, calls=%fused_computation.5 | convolution fusion | flops 4436000768 | bytes 31485952 | tf_op jit(solution)/shard_map/dot_general | solution.py:34
  338.4 8.6 %fusion.29 = (f32[512]{0:T(512)S(1)}, f32[512,1024]{1,0:T(8,128)S(1)}) fusion(f32[1024]{0:T(1024)S(1)} %get-tuple-element.97, bf16[512,4096]{1,0:T(8,128)(2,1)} %get-tuple-element.83, bf16[1024,4096]{1,0:T(8,128)(2,1)} %all-gather.19.cloned.1.call-done, f32[1024]{0:T(1024)S(1)} %get-tuple-element.96, f32[1024]{0:T(1024)S(1)} %get-tuple-element.113, ...), kind=kOutput, calls=%fused_computation.123 | convolution fusion | flops 4298636800 | bytes 16795648 | tf_op jit(solution)/shard_map/dot_general | solution.py:38
  347.4 0.9 fusion.12
  348.3 1.9 fusion.23
  350.5 14.7 %convert_reduce_fusion = (f32[4096]{0:T(1024)S(1)}, bf16[512,4096]{1,0:T(8,128)(2,1)}) fusion(f32[512,4096]{1,0:T(8,128)} %get-tuple-element.84, f32[512,4096]{1,0:T(8,128)} %get-tuple-element.107, f32[4096]{0:T(1024)S(1)} %bitcast.199, bf16[512,1024]{1,0:T(8,128)(2,1)S(1)} %get-tuple-element.76, bf16[1024,4096]{1,0:T(8,128)(2,1)} %all-gather.19.cloned.1.call-done), kind=kOutput, calls=%fused_computation.2 | convolution fusion | flops 4330614784 | bytes 30441472 | tf_op jit(solution)/shard_map/dot_general | solution.py:34
  365.2 7.2 multiply_reduce_fusion
  373.2 1.3 copy-done.7
  374.7 1.0 copy-done.17
  375.7 2.6 convolution_convert_fusion.3
  378.5 9.2 %convolution_convert_fusion.1 = bf16[1024,4096]{1,0:T(8,128)(2,1)} fusion(bf16[512,4096]{1,0:T(8,128)(2,1)} %get-tuple-element.74, f32[512,1024]{1,0:T(8,128)S(1)} %get-tuple-element.106, f32[1024]{0:T(1024)S(1)} %get-tuple-element.96, f32[1024]{0:T(1024)S(1)} %get-tuple-element.113, f32[512]{0:T(512)S(1)} %fusion.17, f32[512]{0:T(512)S(1)} %broadcast_multiply_fusion.1), kind=kOutput, calls=%fused_computation.20 | convolution fusion | flops 4301783040 | bytes 14692352 | tf_op jit(solution)/shard_map/dot_general | solution.py:44
  387.8 9.5 %convolution_convert_fusion = bf16[1024,4096]{1,0:T(8,128)(2,1)} fusion(bf16[512,1024]{1,0:T(8,128)(2,1)S(1)} %get-tuple-element.76, bf16[512,4096]{1,0:T(8,128)(2,1)} %get-tuple-element.83), kind=kOutput, calls=%fused_computation.19 | convolution fusion | flops 4299161600 | bytes 13631488 | tf_op jit(solution)/shard_map/dot_general | solution.py:44
  397.4 1.2 copy-done.18
  398.5 1.0 copy-done.22
  399.6 1.3 convolution_convert_fusion.4
  400.9 27.4 %all_to_all.10 = bf16[4,512,256]{2,1,0:T(8,128)(2,1)S(1)} all-to-all(bf16[4,512,256]{2,1,0:T(8,128)(2,1)S(1)} %bitcast.174), channel_id=1, replica_groups=mesh['dp'=8,'tensor'=4] {'tensor'}, dimensions={0} | all-to-all | bytes 2097152 | tf_op jit(solution)/shard_map/all_to_all | solution.py:343
  428.3 1.4 copy.69.g_t
  429.7 1.5 copy-done.2
  431.2 1.4 copy-done.4
  432.6 66.5 %shard_map.204 = (bf16[256,2048]{1,0:T(8,128)(2,1)S(1)}, bf16[2048,256]{1,0:T(8,128)(2,1)S(1)}, bf16[2048,256]{1,0:T(8,128)(2,1)S(1)}) custom-call(s32[2,8]{1,0:T(2,128)S(1)} %pad_add_fusion.ranges, bf16[256,2048]{1,0:T(8,128)(2,1)S(1)} %copy-done.4, bf16[2048,256]{1,0:T(8,128)(2,1)S(1)} %bitcast.167, bf16[2048,256]{1,0:T(8,128)(2,1)} %copy-done.5, ...), custom_call_target="tpu_custom_call" | custom-call | flops 42949672960 | bytes 8388608 | tf_op jit(solution)/shard_map/pallas_call | solution.py:204
  499.1 2.1 fusion.16
  501.2 2.1 fusion.15
  503.4 4.1 fusion.14
  507.5 1.3 pad_maximum_fusion
  508.8 4.3 copy.74
  513.1 3.2 copy.80
  516.6 2.4 fusion.30
  519.0 1.3 fusion.31
  520.3 3.4 add_convert_fusion
  524.4 44.1 %reduce-scatter.21.cloned.1.call-done = bf16[128,4096]{1,0:T(8,128)(2,1)} async-done(((bf16[1024,4096]{1,0:T(8,128)(2,1)}), bf16[128,4096]{1,0:T(8,128)(2,1)}) %reduce-scatter.21.cloned.1.call-update) | async-done | bytes 1048592 | tf_op jit(solution)/shard_map/reduce_scatter | solution.py:349
  569.2 39.7 %psum.7 = f32[12,1024]{1,0:T(8,128)S(1)} all-reduce(f32[12,1024]{1,0:T(8,128)S(1)} %concatenate.11), channel_id=1, replica_groups=mesh['dp'=8,'tensor'=4] {'dp','tensor'}, use_global_device_ids=true, to_apply=%region_30.31 | all-reduce | flops 12288 | bytes 98304 | tf_op jit(solution)/shard_map/psum | solution.py:402
  610.1 1.5 convert_element_type.193
  611.7 18.9 %reduce-scatter.25.cloned.1.call-done = bf16[128,768]{1,0:T(8,128)(2,1)} async-done(((bf16[1024,768]{1,0:T(8,128)(2,1)}), bf16[128,768]{1,0:T(8,128)(2,1)}) %reduce-scatter.25.cloned.1.call-update) | async-done | bytes 196624
  630.6 1.0 reshape.400
  631.8 0.9 copy.71
  632.7 76.9 %reduce-scatter.11.cloned.1.call-done = bf16[512,1024]{1,0:T(8,128)(2,1)} async-done(((bf16[2048,1024]{1,0:T(8,128)(2,1)}), bf16[512,1024]{1,0:T(8,128)(2,1)}) %reduce-scatter.11.cloned.1.call-update) | async-done | bytes 1048592 | tf_op jit(solution)/shard_map/reduce_scatter | solution.py:365
  709.6 2.5 add_convert_fusion.2
  712.1 27.4 %reduce-scatter.19.cloned.1.call-done = bf16[128,1024]{1,0:T(8,128)(2,1)} async-done(((bf16[128,4096]{1,0:T(8,128)(2,1)}), bf16[128,1024]{1,0:T(8,128)(2,1)}) %reduce-scatter.19.cloned.1.call-update) | async-done | bytes 262160 | tf_op jit(solution)/shard_map/reduce_scatter | solution.py:350
  739.5 1.8 convert_element_type.195
  741.3 26.2 %reduce-scatter.23.cloned.1.call-done = bf16[128,1024]{1,0:T(8,128)(2,1)} async-done(((bf16[128,4096]{1,0:T(8,128)(2,1)}), bf16[128,1024]{1,0:T(8,128)(2,1)}) %reduce-scatter.23.cloned.1.call-update) | async-done | bytes 262160 | tf_op jit(solution)/shard_map/reduce_scatter | solution.py:350
  767.5 1.8 convert_element_type.197
  (133 shorter events, 13.1 us)
Async XLA Ops:
  7.2 37.0 %all-gather.13.cloned.1.call-start = ((), (), s32[]{:S(2)}) async-start(), calls=%async_computation.12 | async-start | bytes 1310720 | tf_op jit(solution)/shard_map/all_gather | solution.py:298
  7.9 64.9 %all-gather.17.cloned.1.call-start = ((), (), s32[]{:S(2)}) async-start(), calls=%async_computation.14 | async-start | bytes 1310720 | tf_op jit(solution)/shard_map/all_gather | solution.py:298
  8.7 92.1 %all-gather.21.cloned.1.call-start = ((), (), s32[]{:S(2)}) async-start(), calls=%async_computation.23 | async-start | bytes 1843200 | tf_op jit(solution)/shard_map/all_gather | solution.py:278
  14.4 168.6 %all-gather.9.cloned.1.call-start = ((), (), s32[]{:S(2)}) async-start(), calls=%async_computation.10 | async-start | bytes 5242880 | tf_op jit(solution)/shard_map/all_gather | solution.py:269
  15.0 265.4 %all-gather.11.cloned.1.call-start = ((), (), s32[]{:S(2)}) async-start(), calls=%async_computation.11 | async-start | bytes 2359296 | tf_op jit(solution)/shard_map/all_gather | solution.py:299
  34.4 276.2 %all-gather.15.cloned.1.call-start = ((), (), s32[]{:S(2)}) async-start(), calls=%async_computation.13 | async-start | bytes 9437184 | tf_op jit(solution)/shard_map/all_gather | solution.py:299
  44.2 294.3 %all-gather.19.cloned.1.call-start = ((), (), s32[]{:S(2)}) async-start(), calls=%async_computation.15 | async-start | bytes 9437184 | tf_op jit(solution)/shard_map/all_gather | solution.py:299
  46.3 154.5 %copy-start = (s32[2048,1]{1,0:T(8,128)}, s32[2048,1]{1,0:T(8,128)S(1)}, u32[]{:S(2)}) copy-start(s32[2048,1]{1,0:T(8,128)S(1)} %copy.64.seg_k) | copy-start | bytes 24580
  104.3 78.7 %copy-start.13 = (bf16[1,8,128,256]{3,2,0,1:T(8,128)(2,1)}, bf16[1,8,128,256]{3,2,0,1:T(8,128)(2,1)S(1)}, u32[]{:S(2)}) copy-start(bf16[1,8,128,256]{3,2,0,1:T(8,128)(2,1)S(1)} %get-tuple-element.88) | copy-start | bytes 1572868
  186.5 5.7 copy-start.1
  187.1 13.7 %copy-start.3 = (bf16[256,2048]{1,0:T(8,128)(2,1)}, bf16[256,2048]{1,0:T(8,128)(2,1)S(1)}, u32[]{:S(2)}) copy-start(bf16[256,2048]{1,0:T(8,128)(2,1)S(1)} %copy.61.q_t) | copy-start | bytes 3145732
  193.6 7.2 copy-start.5
  200.9 1.3 copy-start.6
  273.6 33.3 %copy-start.14 = (bf16[512,1024]{1,0:T(8,128)(2,1)S(1)}, bf16[512,1024]{1,0:T(8,128)(2,1)}, u32[]{:S(2)}) copy-start(bf16[512,1024]{1,0:T(8,128)(2,1)} %param.12) | copy-start | bytes 3145732
  276.5 29.4 %all-to-all-start = ((bf16[4,512,256]{1,2,0:T(8,128)(2,1)}), bf16[4,512,256]{1,2,0:T(8,128)(2,1)S(1)}, u32[]{:S(2)}, u32[]{:S(2)}) async-start(bf16[4,512,256]{1,2,0:T(8,128)(2,1)} %bitcast.165), calls=%async_computation | async-start | bytes 2097152 | tf_op jit(solution)/shard_map/all_to_all | solution.py:321
  280.1 223.2 %reduce-scatter.13.cloned.1.call-start = ((), (), s32[]{:S(2)}) async-start(), calls=%async_computation.17 | async-start | bytes 2359296 | tf_op jit(solution)/shard_map/reduce_scatter | solution.py:349
  305.9 1.0 copy-start.15
  338.4 9.0 %copy-start.10 = (bf16[512,1024]{1,0:T(8,128)(2,1)S(1)}, bf16[512,1024]{1,0:T(8,128)(2,1)}, u32[]{:S(2)}) copy-start(bf16[512,1024]{1,0:T(8,128)(2,1)} %param.23) | copy-start | bytes 3145732
  348.3 16.9 %slice-start = ((s8[8388608]{0:T(1024)(128)(4,1)}), s8[4194304]{0:T(1024)(128)(4,1)S(1)}, s32[]{:S(2)}) async-start(s8[8388608]{0:T(1024)(128)(4,1)} %bitcast.214), calls=%async_computation.25 | async-start | bytes 8388608
  350.4 14.8 %slice-start.1 = ((s8[8388608]{0:T(1024)(128)(4,1)}), s8[4194304]{0:T(1024)(128)(4,1)S(1)}, s32[]{:S(2)}) async-start(s8[8388608]{0:T(1024)(128)(4,1)} %bitcast.214), calls=%async_computation.26 | async-start | bytes 8388608
  372.4 3.3 copy-start.16
  373.2 1.3 copy-start.7
  374.7 1.0 copy-start.17
  378.4 145.5 %reduce-scatter.17.cloned.1.call-start = ((), (), s32[]{:S(2)}) async-start(), calls=%async_computation.19 | async-start | bytes 9437184 | tf_op jit(solution)/shard_map/reduce_scatter | solution.py:349
  387.7 180.8 %reduce-scatter.21.cloned.1.call-start = ((), (), s32[]{:S(2)}) async-start(), calls=%async_computation.21 | async-start | bytes 9437184 | tf_op jit(solution)/shard_map/reduce_scatter | solution.py:349
  397.3 1.2 copy-start.18
  397.3 2.3 copy-start.22
  397.3 212.8 %reduce-scatter.15.cloned.1.call-start = ((), (), s32[]{:S(2)}) async-start(), calls=%async_computation.18 | async-start | bytes 327680 | tf_op jit(solution)/shard_map/reduce_scatter | solution.py:350
  428.3 1.4 copy-start.9
  429.7 1.5 copy-start.2
  431.2 1.4 copy-start.4
  432.6 66.5 %copy-start.21 = (bf16[2048,1024]{1,0:T(8,128)(2,1)S(1)}, bf16[2048,1024]{1,0:T(8,128)(2,1)}, u32[]{:S(2)}) copy-start(bf16[2048,1024]{1,0:T(8,128)(2,1)} %all-gather.9.cloned.1.call-done) | copy-start | bytes 12582916
  503.3 127.3 %reduce-scatter.25.cloned.1.call-start = ((), (), s32[]{:S(2)}) async-start(), calls=%async_computation.24 | async-start | bytes 1769472
  503.3 4.1 copy-start.19
  503.3 4.1 copy-start.20
  516.3 193.3 %reduce-scatter.11.cloned.1.call-start = ((), (), s32[]{:S(2)}) async-start(), calls=%async_computation.16 | async-start | bytes 5242880 | tf_op jit(solution)/shard_map/reduce_scatter | solution.py:365
  516.6 2.4 copy-start.12
  519.0 1.3 copy-start.11
  523.8 215.7 %reduce-scatter.19.cloned.1.call-start = ((), (), s32[]{:S(2)}) async-start(), calls=%async_computation.20 | async-start | bytes 1310720 | tf_op jit(solution)/shard_map/reduce_scatter | solution.py:350
  524.4 243.1 %reduce-scatter.23.cloned.1.call-start = ((), (), s32[]{:S(2)}) async-start(), calls=%async_computation.22 | async-start | bytes 1310720 | tf_op jit(solution)/shard_map/reduce_scatter | solution.py:350
  568.7 140.9 %copy-start.8 = (f32[512,1024]{1,0:T(8,128)S(1)}, f32[512,1024]{1,0:T(8,128)}, u32[]{:S(2)}) copy-start(f32[512,1024]{1,0:T(8,128)} %copy-done.7) | copy-start | bytes 6291460
Sparse Core Ops, SparseCore 0:
  9.6 34.5 all-gather.12
  45.7 27.0 all-gather.16
  75.3 25.4 all-gather.20
  102.2 80.7 all-gather.8
  184.7 26.4 all-gather.10
  212.9 54.3 all-gather.14
  269.3 54.3 all-gather.18
  378.5 40.1 reduce-scatter.12
  422.5 71.3 reduce-scatter.16
  497.2 71.2 reduce-scatter.20
  570.8 19.6 reduce-scatter.14
  593.7 36.7 reduce-scatter.24
  632.8 76.7 reduce-scatter.10
  711.9 27.6 reduce-scatter.18
  741.7 25.7 reduce-scatter.22

commit v2 on v1

--- a/solution.py
+++ b/solution.py
@@ -52,43 +52,43 @@
     local = heads * head_dim
     query = q_t[...]
     rows = lax.broadcasted_iota(jnp.int32, (local, block), 0) // head_dim
-    masked = [jnp.where(rows == h, query, jnp.zeros_like(query)) for h in range(heads)]
-    seg_row = seg_q[0:1, :]
+    wide = jnp.concatenate(
+        [jnp.where(rows == h, query, jnp.zeros_like(query)) for h in range(heads)], 1
+    )
+    seg_row = jnp.concatenate([seg_q[0:1, :]] * heads, 1)
 
     def step(j, carry):
+        peak, total, accs = carry
         at = pl.ds(pl.multiple_of(j * block, block), block)
-        keys = k[at, :]
-        same = seg_k[at, :] == seg_row
+        scores = jnp.dot(k[at, :], wide, preferred_element_type=jnp.float32)
+        scores = jnp.where(seg_k[at, :] == seg_row, scores, -1e30)
+        top = jnp.maximum(peak, jnp.max(scores, 0, keepdims=True))
+        powered = jnp.exp(scores - top)
+        shrink = jnp.exp(peak - top)
+        total = total * shrink + jnp.sum(powered, 0, keepdims=True)
+        powered = powered.astype(jnp.bfloat16)
         new = []
         for h in range(heads):
-            peak, total, acc = carry[h]
-            scores = jnp.dot(keys, masked[h], preferred_element_type=jnp.float32)
-            scores = jnp.where(same, scores, -1e30)
-            top = jnp.maximum(peak, jnp.max(scores, 0, keepdims=True))
-            powered = jnp.exp(scores - top)
-            shrink = jnp.exp(peak - top)
-            total = total * shrink + jnp.sum(powered, 0, keepdims=True)
+            cols = slice(h * block, (h + 1) * block)
             part = jnp.dot(
                 v_t[h * head_dim : (h + 1) * head_dim, at],
-                powered.astype(jnp.bfloat16),
+                powered[:, cols],
                 preferred_element_type=jnp.float32,
             )
-            new.append((top, total, acc * shrink + part))
-        return tuple(new)
-
-    first = tuple(
-        (
-            jnp.full((1, block), -1e30, jnp.float32),
-            jnp.zeros((1, block), jnp.float32),
-            jnp.zeros((head_dim, block), jnp.float32),
-        )
-        for _ in range(heads)
-    )
-    done = lax.fori_loop(low, high, step, first)
+            new.append(accs[h] * shrink[:, cols] + part)
+        return top, total, tuple(new)
+
+    first = (
+        jnp.full((1, heads * block), -1e30, jnp.float32),
+        jnp.zeros((1, heads * block), jnp.float32),
+        tuple(jnp.zeros((head_dim, block), jnp.float32) for _ in range(heads)),
+    )
+    peak, total, accs = lax.fori_loop(low, high, step, first)
+    log_sum = peak + jnp.log(total)
     for h in range(heads):
-        peak, total, acc = done[h]
-        ctx_t[h * head_dim : (h + 1) * head_dim, :] = acc / total
-        lse[h : h + 1, :] = peak + jnp.log(total)
+        cols = slice(h * block, (h + 1) * block)
+        ctx_t[h * head_dim : (h + 1) * head_dim, :] = accs[h] / total[:, cols]
+        lse[h : h + 1, :] = log_sum[:, cols]
 
 
 def backward_kernel(
@@ -109,43 +109,39 @@
     query_t, query, grad_t, grad = q_t[...], q[...], g_t[...], g[...]
     zero_t, zero = jnp.zeros_like(query_t), jnp.zeros_like(query)
     products = grad_t.astype(jnp.float32) * ctx_t[...]
-    inner = [
-        jnp.sum(products[h * head_dim : (h + 1) * head_dim, :], 0, keepdims=True)
-        for h in range(heads)
-    ]
-    qs_t = [jnp.where(rows == h, query_t, zero_t) for h in range(heads)]
-    gs_t = [jnp.where(rows == h, grad_t, zero_t) for h in range(heads)]
-    qs = [jnp.where(lanes == h, query, zero) for h in range(heads)]
-    gs = [jnp.where(lanes == h, grad, zero) for h in range(heads)]
-    seg_row = seg_q[0:1, :]
+    inner = jnp.concatenate(
+        [
+            jnp.sum(products[h * head_dim : (h + 1) * head_dim, :], 0, keepdims=True)
+            for h in range(heads)
+        ],
+        1,
+    )
+    qs_t = jnp.concatenate([jnp.where(rows == h, query_t, zero_t) for h in range(heads)], 1)
+    gs_t = jnp.concatenate([jnp.where(rows == h, grad_t, zero_t) for h in range(heads)], 1)
+    qs = jnp.concatenate([jnp.where(lanes == h, query, zero) for h in range(heads)], 0)
+    gs = jnp.concatenate([jnp.where(lanes == h, grad, zero) for h in range(heads)], 0)
+    logs = jnp.concatenate([lse[h : h + 1, :] for h in range(heads)], 1)
+    seg_row = jnp.concatenate([seg_q[0:1, :]] * heads, 1)
 
     def step(j, carry):
         at = pl.ds(pl.multiple_of(j * block, block), block)
-        keys, vals = k[at, :], v[at, :]
-        same = seg_k[at, :] == seg_row
-        new = []
-        d_keys = jnp.zeros((block, local), jnp.float32)
-        d_vals = jnp.zeros((block, local), jnp.float32)
-        for h in range(heads):
-            scores = jnp.dot(keys, qs_t[h], preferred_element_type=jnp.float32)
-            weights = jnp.exp(jnp.where(same, scores - lse[h : h + 1, :], -1e30))
-            d_weights = jnp.dot(vals, gs_t[h], preferred_element_type=jnp.float32)
-            d_scores = (weights * (d_weights - inner[h])).astype(jnp.bfloat16)
-            d_vals += jnp.dot(
-                weights.astype(jnp.bfloat16), gs[h], preferred_element_type=jnp.float32
+        scores = jnp.dot(k[at, :], qs_t, preferred_element_type=jnp.float32)
+        weights = jnp.exp(jnp.where(seg_k[at, :] == seg_row, scores - logs, -1e30))
+        d_weights = jnp.dot(v[at, :], gs_t, preferred_element_type=jnp.float32)
+        d_scores = (weights * (d_weights - inner)).astype(jnp.bfloat16)
+        dv_sum[at, :] += jnp.dot(
+            weights.astype(jnp.bfloat16), gs, preferred_element_type=jnp.float32
+        )
+        dk_sum[at, :] += jnp.dot(d_scores, qs, preferred_element_type=jnp.float32)
+        return tuple(
+            carry[h]
+            + jnp.dot(
+                k_t[h * head_dim : (h + 1) * head_dim, at],
+                d_scores[:, h * block : (h + 1) * block],
+                preferred_element_type=jnp.float32,
             )
-            d_keys += jnp.dot(d_scores, qs[h], preferred_element_type=jnp.float32)
-            new.append(
-                carry[h]
-                + jnp.dot(
-                    k_t[h * head_dim : (h + 1) * head_dim, at],
-                    d_scores,
-                    preferred_element_type=jnp.float32,
-                )
-            )
-        dk_sum[at, :] += d_keys
-        dv_sum[at, :] += d_vals
-        return tuple(new)
+            for h in range(heads)
+        )
 
     first = tuple(jnp.zeros((head_dim, block), jnp.float32) for _ in range(heads))
     done = lax.fori_loop(low, high, step, first)
@@ -258,9 +254,7 @@
     members = lax.axis_size("tensor")
     groups = lax.axis_size("dp")
     position = lax.axis_index("tensor")
-    place = lax.axis_index("dp")
     part, local = w_qkv.shape[1:]
-    hidden_all = w_in.shape[1] * members
     block = 256
 
     vectors = jnp.concatenate(
@@ -276,6 +270,12 @@
         ]
     )
     packed = lax.all_gather(packed, "dp", axis=0, tiled=False)
+    shared = jnp.concatenate([w_attn_out.reshape(-1, w_in.shape[1]), w_in, w_out])
+    shared = lax.all_to_all(
+        jnp.broadcast_to(shared, (members, *shared.shape)),
+        "tensor", split_axis=0, concat_axis=0, tiled=False,
+    )
+    inputs, packed, shared = lax.optimization_barrier((inputs, packed, shared))
     qkv_all = (
         packed[:, : 3 * part]
         .reshape(groups, 3, part, local)
@@ -294,11 +294,15 @@
     query_bias = lax.dynamic_slice_in_dim(qv_bias[0], position * local, local)
     value_bias = lax.dynamic_slice_in_dim(qv_bias[1], position * local, local)
 
+    top = shared.shape[1] - 2 * part
+
     def everywhere(w):
-        w = lax.all_gather(w, "tensor", axis=1, tiled=True)
+        w = w.reshape(members, part, -1).transpose(1, 0, 2).reshape(part, -1)
         return lax.all_gather(w, "dp", axis=0, tiled=True)
 
-    attn_out_all, in_all, out_all = everywhere(w_attn_out), everywhere(w_in), everywhere(w_out)
+    attn_out_all = everywhere(shared[:, :top])
+    in_all = everywhere(shared[:, top : top + part])
+    out_all = everywhere(shared[:, top + part :])
 
     segments = segment_ids(doc_lengths, LEN)[0]
     seg_k = segments[:, None]
@@ -345,14 +349,16 @@
         "tensor", split_axis=0, concat_axis=0, tiled=False,
     ).reshape(rows_here * members, local)
 
-    def owned(grad):
+    def halves(grad):
         grad = lax.psum_scatter(grad.astype(low), "dp", scatter_dimension=0, tiled=True)
-        grad = lax.psum_scatter(grad, "tensor", scatter_dimension=1, tiled=True)
-        return grad.astype(jnp.float32)
-
-    grad_in = owned(matmul_tn(normed, grad_pre))
-    grad_out = owned(matmul_tn(grad_mixed, activated))
-    grad_attn_out = owned(matmul_tn(grad_attended, context))
+        return grad.reshape(part, members, -1).transpose(1, 0, 2)
+
+    grad_out = halves(matmul_tn(grad_mixed, activated))
+    grad_in = halves(matmul_tn(normed, grad_pre))
+    both = lax.psum_scatter(
+        jnp.concatenate([grad_in, grad_out], 1), "tensor", scatter_dimension=0, tiled=False
+    ).astype(jnp.float32)
+    grad_in, grad_out = both[:part], both[part:]
 
     grad_queries_t, grad_keys, grad_values = attend_backward(
         ranges, queries_t, queries, keys, keys_t, values, grad_context.T, grad_context,
@@ -361,49 +367,73 @@
     total = dot(grad_queries_t, qkv_all[0], 0, 1)
     total = total + matmul_nt(grad_keys, qkv_all[1])
     total = total + matmul_nt(grad_values, qkv_all[2])
-    grad_tokens = (
-        lax.psum_scatter(
-            total.astype(low), "tensor", scatter_dimension=0, tiled=True
-        ).astype(jnp.float32)
-        + grad_one
-    ).astype(low)
-    grad_qkv = jnp.stack(
-        [
-            dot(inputs, grad_queries_t, 0, 1),
-            matmul_tn(inputs, grad_keys),
-            matmul_tn(inputs, grad_values),
-        ]
-    ).astype(low)
-    grad_qkv = lax.psum_scatter(grad_qkv, "dp", scatter_dimension=1, tiled=True)
-    grad_qkv = grad_qkv.astype(jnp.float32)
+    total = total.astype(low)
 
     def placed(piece):
         return lax.dynamic_update_slice_in_dim(
             jnp.zeros((width,), jnp.float32), piece, position * local, 0
         )
 
+    sums = jnp.stack(
+        [
+            placed(jnp.sum(grad_queries_t.astype(jnp.float32), 1)),
+            placed(column_sum(grad_values)),
+            column_sum(grad_attended),
+            column_sum(grad_mixed),
+            gain_one,
+            gain_two,
+            shift_one,
+            shift_two,
+        ]
+    )
     sums = jnp.concatenate(
         [
-            jnp.stack(
-                [
-                    placed(jnp.sum(grad_queries_t.astype(jnp.float32), 1)),
-                    placed(column_sum(grad_values)),
-                    column_sum(grad_attended),
-                    column_sum(grad_mixed),
-                    gain_one,
-                    gain_two,
-                    shift_one,
-                    shift_two,
-                ]
-            ),
-            column_sum(grad_pre).reshape(-1, width),
-        ]
-    )
-    sums = lax.psum(sums, ("dp", "tensor"))
-    pieces = lax.dynamic_slice_in_dim(sums[:8], place * part, part, 1)
-    grad_hidden = lax.dynamic_slice_in_dim(
-        sums[8:].reshape(-1), place * b_hidden.size, b_hidden.size, 0
-    )
+            sums.reshape(8, groups, part).transpose(1, 0, 2).reshape(groups, 8 * part),
+            column_sum(grad_pre).reshape(groups, -1),
+        ],
+        1,
+    ).astype(low)
+    amount = sums.shape[1]
+    last = jnp.concatenate(
+        [
+            dot(inputs, grad_queries_t, 0, 1).astype(low),
+            matmul_tn(inputs, grad_keys).astype(low),
+            matmul_tn(inputs, grad_values).astype(low),
+            matmul_tn(grad_attended, context).astype(low),
+        ],
+        1,
+    )
+    across = last.shape[1]
+    extra = -(-amount // across)
+    extra += -extra % 16
+    sums = jnp.pad(sums, ((0, 0), (0, extra * across - amount)))
+    last = jnp.concatenate(
+        [last.reshape(groups, part, across), sums.reshape(groups, extra, across)], 1
+    )
+    total, last = lax.optimization_barrier((total, last))
+    last = lax.psum_scatter(last, "dp", scatter_dimension=0, tiled=False)
+    total = lax.all_to_all(
+        total.reshape(members, rows_here, width),
+        "tensor", split_axis=0, concat_axis=0, tiled=False,
+    )
+    grad_tokens = (jnp.sum(total.astype(jnp.float32), 0) + grad_one).astype(low)
+    grad_qkv = last[:part, : 3 * local].reshape(part, 3, local).transpose(1, 0, 2)
+    grad_qkv = grad_qkv.astype(jnp.float32)
+    sums = last[part:].reshape(-1)[:amount]
+    lines = -(-amount // local)
+    sums = jnp.pad(sums, (0, lines * local - amount)).reshape(1, lines, local)
+    final = jnp.concatenate(
+        [
+            last[:part, 3 * local :].reshape(part, members, local).transpose(1, 0, 2),
+            jnp.broadcast_to(sums, (members, lines, local)),
+        ],
+        1,
+    )
+    final = lax.all_to_all(final, "tensor", split_axis=0, concat_axis=0, tiled=False)
+    final = jnp.sum(final.astype(jnp.float32), 0)
+    grad_attn_out = final[:part]
+    sums = final[part:].reshape(-1)[:amount]
+    pieces = sums[: 8 * part].reshape(8, part)
     return (
         output.astype(low),
         grad_tokens,
@@ -413,7 +443,7 @@
         grad_out,
         pieces[0:2],
         pieces[2:4],
-        grad_hidden,
+        sums[8 * part :],
         pieces[4:6],
         pieces[6:8],
     )

time: 785 us -> 618 us (0.79)
  blocking collectives: 86.4 us -> 0 us
  waiting for transfers between devices: 364 us -> 294 us
  Pallas kernels: 138 us -> 86.3 us
  local copies, waits for them, and re-layouts: 35.6 us -> 54.4 us
  starting transfers between devices: 4.5 us -> 22.7 us
    all_to_all x0 -> x4, waiting for transfers between devices: none -> 152 us  [the longest x1 70.8 us: on_device(): lax.all_to_all(jnp.broadcast_to(shared, (members, *shared.shape)), 'tenso...]
    reduce_scatter x7 -> x4, waiting for transfers between devices: 175 us -> 53.1 us  [the longest x1 51.6 us: on_device(): last = lax.psum_scatter(last, 'dp', scatter_dimension=0, tiled=False)]
    all_gather x1, waiting for transfers between devices: 78.7 us -> 32.7 us  [on_device(): inputs = lax.all_gather(tokens, 'tensor', axis=0, tiled=True)]
    psum x1 -> x0, blocking collectives: 39.7 us -> none  [on_device(): sums = lax.psum(sums, ('dp', 'tensor'))]
    all_gather x2 -> x0, waiting for transfers between devices: 36 us -> none  [everywhere(): w = lax.all_gather(w, 'tensor', axis=1, tiled=True)]
    pallas_call x1, Pallas kernels: 71.4 us -> 37.4 us  [attend_forward(): pl.pallas_call(functools.partial(forward_kernel, heads, head_dim, block),...]
    all_to_all x1 -> x0, blocking collectives: 27.4 us -> none  [on_device(): lax.all_to_all(grad_context.reshape(rows_here, members, local).transpose(...]
    unnamed x16 -> x9, waiting for transfers between devices: 21.5 us -> 0.83 us
  transfers between devices with their start and end apart: 16 -> 14, of which waited for: 10 -> 10; matrix products, arithmetic and copies ran while one was open for 15% -> 25% of each run, Pallas kernels for 18% -> 14%
where the time goes in v2:
time: 618 us; the launch traced here: 606 us
  waiting for transfers between devices  294 us (48%)
  matrix products  108 us (17%)
  Pallas kernels  86.3 us (14%)
  local copies, waits for them, and re-layouts  54.4 us (9%)
  other arithmetic  26.1 us (4%)
  starting transfers between devices  22.7 us (4%)
  between operations  14.7 us (2%)
    all_to_all x1, waiting for transfers between devices, on_device(): lax.all_to_all(jnp.broadcast_to(shared, (members, *shared.shape)), 'tenso...  70.8 us
    all_to_all x1, waiting for transfers between devices, on_device(): lax.all_to_all(total.reshape(members, rows_here, width), 'tensor', split_...  64.4 us
    dot_general x6, matrix products, matmul(): return jnp.dot(left, right, preferred_element_type=jnp.float32)  57.4 us
    reduce_scatter x1, waiting for transfers between devices, on_device(): last = lax.psum_scatter(last, 'dp', scatter_dimension=0, tiled=False)  51.6 us
    pallas_call x1, Pallas kernels, attend_backward(): pl.pallas_call(functools.partial(backward_kernel, heads, head_dim, block)...  48.8 us
    pallas_call x1, Pallas kernels, attend_forward(): pl.pallas_call(functools.partial(forward_kernel, heads, head_dim, block),...  37.4 us
    all_gather x1, waiting for transfers between devices, on_device(): inputs = lax.all_gather(tokens, 'tensor', axis=0, tiled=True)  32.7 us
    all_to_all x1, waiting for transfers between devices, on_device(): lax.all_to_all(context_t.T.astype(low).reshape(members, rows_here, local)...  26.1 us
  transfers between devices with their start and end apart: 14, of which 10 were waited for; matrix products, arithmetic and copies ran while one was open for 25% of the time, Pallas kernels for 14%

profile of v2, /device:TPU:0, one launch (start us, length us, event | category | flops | bytes accessed | tf_op | source)
XLA Modules:
  0.0 606.1 jit_solution(15202639873716389105)
XLA Ops:
  11.3 1.6 pad_maximum_fusion.5
  14.6 1.1 pad_maximum_fusion.3
  15.7 1.7 broadcast_in_dim.32
  17.4 6.3 %all-to-all-start = ((bf16[4,288,1024]{2,1,0:T(8,128)(2,1)}), bf16[4,288,1024]{2,1,0:T(8,128)(2,1)S(1)}, u32[]{:S(2)}, u32[]{:S(2)}) async-start(bf16[4,288,1024]{2,1,0:T(8,128)(2,1)} %broadcast_in_dim.32), calls=%async_computation | async-start | bytes 4718592 | tf_op jit(solution)/shard_map/all_to_all | solution.py:274
  23.7 18.1 %all-gather.15.cloned.1.call-done = bf16[3200,256]{1,0:T(8,128)(2,1)} async-done(((bf16[400,256]{1,0:T(8,128)(2,1)}), bf16[3200,256]{1,0:T(8,128)(2,1)}) %all-gather.15.cloned.1.call-update) | async-done | bytes 1638416 | tf_op jit(solution)/shard_map/all_gather | solution.py:272
  41.8 70.8 %all-to-all-done = bf16[4,288,1024]{2,1,0:T(8,128)(2,1)S(1)} async-done(((bf16[4,288,1024]{2,1,0:T(8,128)(2,1)}), bf16[4,288,1024]{2,1,0:T(8,128)(2,1)S(1)}, u32[]{:S(2)}, u32[]{:S(2)}) %all-to-all-start) | async-done | bytes 2359328 | tf_op jit(solution)/shard_map/all_to_all | solution.py:274
  112.6 32.7 %all-gather.7.cloned.1.call-done = bf16[2048,1024]{1,0:T(8,128)(2,1)} async-done(((bf16[512,1024]{1,0:T(8,128)(2,1)}), bf16[2048,1024]{1,0:T(8,128)(2,1)}) %all-gather.7.cloned.1.call-update) | async-done | bytes 4194320 | tf_op jit(solution)/shard_map/all_gather | solution.py:263
  146.4 2.8 copy.96
  149.2 4.3 fusion.28
  154.5 1.8 slice.151
  157.3 1.1 fusion.29
  158.4 3.6 fusion.10.q
  162.7 4.9 convolution_convert_fusion.2
  167.6 2.3 copy.91.k
  169.9 4.7 fusion.7.v
  174.6 2.3 copy.92.v_t
  176.9 1.2 copy-done.6
  178.1 37.4 %shard_map.203 = (f32[256,2048]{1,0:T(8,128)}, f32[8,2048]{1,0:T(8,128)S(1)}) custom-call(s32[2,8]{1,0:T(2,128)S(1)} %pad_add_fusion.ranges, bf16[256,2048]{1,0:T(8,128)(2,1)S(1)} %copy.90.q_t, bf16[2048,256]{1,0:T(8,128)(2,1)S(1)} %copy-done.5, bf16[256,2048]{1,0:T(8,128)(2,1)S(1)} %copy-done.6, s32[8,2048]{1,0:T(8,128)S(1)} %broadcast_in_dim.58.seg_q, ...), custom_call_target="tpu_custom_call" | custom-call | flops 17179869184 | bytes 4194304 | tf_op jit(solution)/shard_map/pallas_call | solution.py:168
  215.6 1.8 convert_element_type.181
  217.4 1.1 copy.129
  218.5 3.5 all-to-all-start.1
  222.1 26.1 %all-to-all-done.1 = bf16[4,512,256]{1,2,0:T(8,128)(2,1)S(1)} async-done(((bf16[4,512,256]{1,2,0:T(8,128)(2,1)}), bf16[4,512,256]{1,2,0:T(8,128)(2,1)S(1)}, u32[]{:S(2)}, u32[]{:S(2)}) %all-to-all-start.1) | async-done | bytes 1048608 | tf_op jit(solution)/shard_map/all_to_all | solution.py:325
  249.2 3.3 fusion.32
  252.9 27.9 %multiply_convert_fusion = (bf16[512,4096]{1,0:T(8,128)(2,1)}, f32[512,4096]{1,0:T(8,128)}, f32[512,4096]{1,0:T(8,128)}) fusion(f32[4096]{0:T(1024)S(1)} %bitcast.247, bf16[1024,4096]{0,1:T(8,128)(2,1)} %all-gather.11.cloned.1.call-done, f32[512,1024]{1,0:T(8,128)S(1)} %get-tuple-element.119, f32[1024]{0:T(1024)S(1)} %get-tuple-element.113, ...), kind=kOutput, calls=%fused_computation.5 | convolution fusion | flops 4436000768 | bytes 31485952 | tf_op jit(solution)/shard_map/dot_general | solution.py:34
  280.8 11.0 %all-gather.13.cloned.1.call-done = bf16[1024,4096]{0,1:T(8,128)(2,1)} async-done(((bf16[128,4096]{0,1:T(8,128)(2,1)}), bf16[1024,4096]{0,1:T(8,128)(2,1)}) %all-gather.13.cloned.1.call-update) | async-done | bytes 8388624 | tf_op jit(solution)/shard_map/all_gather | solution.py:301
  291.8 8.5 %fusion.33 = (f32[512]{0:T(512)S(1)}, f32[512,1024]{1,0:T(8,128)S(1)}) fusion(f32[1024]{0:T(1024)S(1)} %get-tuple-element.114, bf16[512,4096]{1,0:T(8,128)(2,1)} %get-tuple-element.92, bf16[1024,4096]{0,1:T(8,128)(2,1)} %all-gather.13.cloned.1.call-done, f32[1024]{0:T(1024)S(1)} %get-tuple-element.113, f32[1024]{0:T(1024)S(1)} %get-tuple-element.124, ...), kind=kOutput, calls=%fused_computation.145 | convolution fusion | flops 4298636800 | bytes 16795648 | tf_op jit(solution)/shard_map/dot_general | solution.py:38
  301.7 1.9 fusion.26
  303.5 1.3 copy-done.10
  306.1 6.7 %convolution_convert_fusion = bf16[1024,4096]{1,0:T(8,128)(2,1)} fusion(bf16[512,1024]{1,0:T(8,128)(2,1)S(1)} %get-tuple-element.83, bf16[512,4096]{1,0:T(8,128)(2,1)S(1)} %copy-done.25), kind=kOutput, calls=%fused_computation.19 | convolution fusion | flops 4299161600 | bytes 13631488 | tf_op jit(solution)/shard_map/dot_general | solution.py:44
  312.8 14.9 %fusion.24 = (bf16[4096]{0:T(1024)(128)(2,1)S(1)}, bf16[512,4096]{1,0:T(8,128)(2,1)S(1)}) fusion(f32[512,4096]{1,0:T(8,128)} %get-tuple-element.93, f32[512,4096]{1,0:T(8,128)} %get-tuple-element.120, f32[4096]{0:T(1024)S(1)} %bitcast.248, bf16[512,1024]{1,0:T(8,128)(2,1)} %copy-done.22, bf16[1024,4096]{0,1:T(8,128)(2,1)} %all-gather.13.cloned.1.call-done), kind=kOutput, calls=%fused_computation.137 | convolution fusion | flops 4328517632 | bytes 30433280 | tf_op jit(solution)/shard_map/dot_general | solution.py:34
  327.8 9.2 %multiply_reduce_fusion = (bf16[1024]{0:T(1024)(128)(2,1)S(1)}, f32[512]{0:T(512)S(1)}, bf16[1024]{0:T(1024)(128)(2,1)S(1)}, f32[512,1024]{1,0:T(8,128)S(1)}) fusion(f32[512,1024]{1,0:T(8,128)S(1)} %get-tuple-element.119, f32[512]{0:T(512)S(1)} %fusion.17, f32[512]{0:T(512)S(1)} %broadcast_multiply_fusion.1, f32[1024]{0:T(1024)S(1)} %get-tuple-element.124, ...), kind=kOutput, calls=%fused_computation.39 | convolution fusion | flops 4300207616 | bytes 18890752 | tf_op jit(solution)/shard_map/dot_general | solution.py:38
  338.0 1.3 copy-done.16
  339.3 1.3 convolution_convert_fusion.4
  341.7 4.2 all-to-all-start.2
  346.2 9.5 %convolution_convert_fusion.1 = bf16[1024,4096]{1,0:T(8,128)(2,1)} fusion(bf16[512,4096]{1,0:T(8,128)(2,1)} %copy-done.26, f32[512,1024]{1,0:T(8,128)S(1)} %get-tuple-element.119, f32[1024]{0:T(1024)S(1)} %get-tuple-element.113, f32[1024]{0:T(1024)S(1)} %get-tuple-element.124, f32[512]{0:T(512)S(1)} %fusion.17, f32[512]{0:T(512)S(1)} %broadcast_multiply_fusion.1), kind=kOutput, calls=%fused_computation.20 | convolution fusion | flops 4301783040 | bytes 14692352 | tf_op jit(solution)/shard_map/dot_general | solution.py:44
  355.8 1.2 copy-done.14
  357.2 2.6 convolution_convert_fusion.3
  359.8 12.5 %all-to-all-done.2 = bf16[4,512,256]{2,1,0:T(8,128)(2,1)} async-done(((bf16[4,512,256]{2,1,0:T(8,128)(2,1)}), bf16[4,512,256]{2,1,0:T(8,128)(2,1)}, u32[]{:S(2)}, u32[]{:S(2)}) %all-to-all-start.2) | async-done | bytes 1048608 | tf_op jit(solution)/shard_map/all_to_all | solution.py:347
  372.4 2.4 copy.101.g_t
  374.8 1.2 copy-done.2
  376.0 1.2 copy-done.4
  377.3 48.8 %shard_map.204 = (bf16[256,2048]{1,0:T(8,128)(2,1)S(1)}, bf16[2048,256]{1,0:T(8,128)(2,1)S(1)}, bf16[2048,256]{1,0:T(8,128)(2,1)S(1)}) custom-call(s32[2,8]{1,0:T(2,128)S(1)} %pad_add_fusion.ranges, bf16[256,2048]{1,0:T(8,128)(2,1)S(1)} %copy-done.4, bf16[2048,256]{1,0:T(8,128)(2,1)S(1)} %copy-done.2, bf16[2048,256]{1,0:T(8,128)(2,1)} %copy.91.k, ...), custom_call_target="tpu_custom_call" | custom-call | flops 42949672960 | bytes 8388608 | tf_op jit(solution)/shard_map/pallas_call | solution.py:200
  427.7 1.3 convolution_convert_fusion.6
  429.0 1.3 convolution_convert_fusion.5
  430.3 1.3 convolution_convert_fusion.7
  431.9 2.1 pad_maximum_fusion.1
  434.1 5.9 copy.110
  439.9 4.4 pad_maximum_fusion
  444.3 2.6 fusion.34
  446.9 1.3 fusion.35
  448.2 3.4 add_convert_fusion
  451.7 4.9 all-to-all-start.3
  456.6 1.3 copy.126
  458.0 1.5 reduce-scatter.7.cloned.1.call-done
  459.4 1.3 copy.127
  460.7 1.5 pad_maximum_fusion.2
  462.3 51.6 %reduce-scatter.5.cloned.1.call-done = bf16[1,144,1792]{2,1,0:T(8,128)(2,1)} async-done(((bf16[8,144,1792]{2,1,0:T(8,128)(2,1)}), bf16[1,144,1792]{2,1,0:T(8,128)(2,1)}) %reduce-scatter.5.cloned.1.call-update) | async-done | bytes 516112 | tf_op jit(solution)/shard_map/reduce_scatter | solution.py:414
  518.8 64.4 %all-to-all-done.3 = bf16[4,512,1024]{2,1,0:T(8,128)(2,1)} async-done(((bf16[4,512,1024]{2,1,0:T(8,128)(2,1)}), bf16[4,512,1024]{2,1,0:T(8,128)(2,1)}, u32[]{:S(2)}, u32[]{:S(2)}) %all-to-all-start.3) | async-done | bytes 4194336 | tf_op jit(solution)/shard_map/all_to_all | solution.py:415
  583.2 3.5 all-to-all-start.4
  586.6 3.4 convert_reduce_fusion
  590.1 1.2 add_convert_fusion.2
  591.3 4.0 all-to-all-done.4
  597.2 1.1 convert_element_type.221
  598.3 1.1 slice_bitcast_fusion
  (152 shorter events, 24.7 us)
Async XLA Ops:
  7.2 34.6 %all-gather.15.cloned.1.call-start = ((), (), s32[]{:S(2)}) async-start(), calls=%async_computation.17 | async-start | bytes 1843200 | tf_op jit(solution)/shard_map/all_gather | solution.py:272
  12.9 132.4 %all-gather.7.cloned.1.call-start = ((), (), s32[]{:S(2)}) async-start(), calls=%async_computation.9 | async-start | bytes 5242880 | tf_op jit(solution)/shard_map/all_gather | solution.py:263
  17.4 95.2 %all-to-all-start = ((bf16[4,288,1024]{2,1,0:T(8,128)(2,1)}), bf16[4,288,1024]{2,1,0:T(8,128)(2,1)S(1)}, u32[]{:S(2)}, u32[]{:S(2)}) async-start(bf16[4,288,1024]{2,1,0:T(8,128)(2,1)} %broadcast_in_dim.32), calls=%async_computation | async-start | bytes 4718592 | tf_op jit(solution)/shard_map/all_to_all | solution.py:274
  23.7 224.5 %all-gather.9.cloned.1.call-start = ((), (), s32[]{:S(2)}) async-start(), calls=%async_computation.10 | async-start | bytes 2359296 | tf_op jit(solution)/shard_map/all_gather | solution.py:301
  146.4 7.2 %copy-start.24 = (s32[1,4]{1,0:T(1,128)S(1)}, s32[1,4]{1,0:T(1,128)}, u32[]{:S(2)}) copy-start(s32[1,4]{1,0:T(1,128)} %param.22) | copy-start | bytes 52
  146.4 106.6 %all-gather.11.cloned.1.call-start = ((), (), s32[]{:S(2)}) async-start(), calls=%async_computation.11 | async-start | bytes 9437184 | tf_op jit(solution)/shard_map/all_gather | solution.py:301
  153.5 138.3 %all-gather.13.cloned.1.call-start = ((), (), s32[]{:S(2)}) async-start(), calls=%async_computation.12 | async-start | bytes 9437184 | tf_op jit(solution)/shard_map/all_gather | solution.py:301
  154.4 22.5 %copy-start = (s32[2048,1]{1,0:T(8,128)}, s32[2048,1]{1,0:T(8,128)S(1)}, u32[]{:S(2)}) copy-start(s32[2048,1]{1,0:T(8,128)S(1)} %copy.93.seg_k) | copy-start | bytes 24580
  158.4 3.6 copy-start.19
  162.0 5.6 copy-start.1
  162.7 14.2 %copy-start.3 = (bf16[256,2048]{1,0:T(8,128)(2,1)}, bf16[256,2048]{1,0:T(8,128)(2,1)S(1)}, u32[]{:S(2)}) copy-start(bf16[256,2048]{1,0:T(8,128)(2,1)S(1)} %copy.90.q_t) | copy-start | bytes 3145732
  169.9 7.0 %copy-start.5 = (bf16[2048,256]{1,0:T(8,128)(2,1)S(1)}, bf16[2048,256]{1,0:T(8,128)(2,1)}, u32[]{:S(2)}) copy-start(bf16[2048,256]{1,0:T(8,128)(2,1)} %copy.91.k) | copy-start | bytes 3145732
  176.9 1.2 copy-start.6
  215.5 33.7 %copy-start.12 = (bf16[512,1024]{1,0:T(8,128)(2,1)S(1)}, bf16[512,1024]{1,0:T(8,128)(2,1)}, u32[]{:S(2)}) copy-start(bf16[512,1024]{1,0:T(8,128)(2,1)} %param.12) | copy-start | bytes 3145732
  218.5 29.7 %all-to-all-start.1 = ((bf16[4,512,256]{1,2,0:T(8,128)(2,1)}), bf16[4,512,256]{1,2,0:T(8,128)(2,1)S(1)}, u32[]{:S(2)}, u32[]{:S(2)}) async-start(bf16[4,512,256]{1,2,0:T(8,128)(2,1)} %bitcast.204), calls=%async_computation.1 | async-start | bytes 2097152 | tf_op jit(solution)/shard_map/all_to_all | solution.py:325
  222.0 234.6 %reduce-scatter.9.cloned.1.call-start = ((), (), s32[]{:S(2)}) async-start(), calls=%async_computation.15 | async-start | bytes 9437184 | tf_op jit(solution)/shard_map/reduce_scatter | solution.py:353
  248.2 1.0 copy-start.13
  291.8 8.9 %copy-start.9 = (bf16[512,1024]{1,0:T(8,128)(2,1)S(1)}, bf16[512,1024]{1,0:T(8,128)(2,1)}, u32[]{:S(2)}) copy-start(bf16[512,1024]{1,0:T(8,128)(2,1)} %param.23) | copy-start | bytes 3145732
  301.7 4.4 copy-start.25
  303.5 1.3 copy-start.10
  305.1 1.0 copy-start.22
  312.8 14.9 %copy-start.11 = (f32[512,1024]{1,0:T(8,128)S(1)}, f32[512,1024]{1,0:T(8,128)}, u32[]{:S(2)}) copy-start(f32[512,1024]{1,0:T(8,128)} %copy-done.10) | copy-start | bytes 6291460
  327.8 9.2 %copy-start.26 = (bf16[512,4096]{1,0:T(8,128)(2,1)}, bf16[512,4096]{1,0:T(8,128)(2,1)S(1)}, u32[]{:S(2)}) copy-start(bf16[512,4096]{1,0:T(8,128)(2,1)S(1)} %get-tuple-element.87) | copy-start | bytes 12582916
  337.0 2.4 copy-start.16
  337.7 2.9 copy-start.7
  338.0 2.7 copy-start.20
  341.7 30.7 %all-to-all-start.2 = ((bf16[4,512,256]{2,1,0:T(8,128)(2,1)}), bf16[4,512,256]{2,1,0:T(8,128)(2,1)}, u32[]{:S(2)}, u32[]{:S(2)}) async-start(bf16[4,512,256]{2,1,0:T(8,128)(2,1)} %bitcast.213), calls=%async_computation.2 | async-start | bytes 2097152 | tf_op jit(solution)/shard_map/all_to_all | solution.py:347
  345.9 113.5 %reduce-scatter.7.cloned.1.call-start = ((), (), s32[]{:S(2)}) async-start(), calls=%async_computation.14 | async-start | bytes 9437184 | tf_op jit(solution)/shard_map/reduce_scatter | solution.py:353
  355.7 1.2 copy-start.14
  355.7 1.5 copy-start.21
  355.7 158.2 %reduce-scatter.5.cloned.1.call-start = ((), (), s32[]{:S(2)}) async-start(), calls=%async_computation.13 | async-start | bytes 4644864 | tf_op jit(solution)/shard_map/reduce_scatter | solution.py:414
  374.8 1.2 copy-start.2
  376.0 1.2 copy-start.4
  377.3 50.4 %copy-start.23 = (bf16[2048,1024]{1,0:T(8,128)(2,1)S(1)}, bf16[2048,1024]{1,0:T(8,128)(2,1)}, u32[]{:S(2)}) copy-start(bf16[2048,1024]{1,0:T(8,128)(2,1)} %all-gather.7.cloned.1.call-done) | copy-start | bytes 12582916
  430.3 1.7 copy-start.15
  444.3 2.6 copy-start.18
  446.9 1.3 copy-start.17
  451.7 131.5 %all-to-all-start.3 = ((bf16[4,512,1024]{2,1,0:T(8,128)(2,1)}), bf16[4,512,1024]{2,1,0:T(8,128)(2,1)}, u32[]{:S(2)}, u32[]{:S(2)}) async-start(bf16[4,512,1024]{2,1,0:T(8,128)(2,1)} %bitcast.209), calls=%async_computation.3 | async-start | bytes 8388608 | tf_op jit(solution)/shard_map/all_to_all | solution.py:415
  456.6 140.6 %reduce-scatter.11.cloned.1.call-start = ((), (), s32[]{:S(2)}) async-start(), calls=%async_computation.16 | async-start | bytes 2621440 | tf_op jit(solution)/shard_map/reduce_scatter | solution.py:358
  516.9 73.1 %copy-start.8 = (f32[512,1024]{1,0:T(8,128)S(1)}, f32[512,1024]{1,0:T(8,128)}, u32[]{:S(2)}) copy-start(f32[512,1024]{1,0:T(8,128)} %copy-done.7) | copy-start | bytes 6291460
  583.2 12.1 %all-to-all-start.4 = ((bf16[4,134,256]{2,1,0:T(8,128)(2,1)}), bf16[4,134,256]{2,1,0:T(8,128)(2,1)S(1)}, u32[]{:S(2)}, u32[]{:S(2)}) async-start(bf16[4,134,256]{2,1,0:T(8,128)(2,1)} %pad_maximum_fusion.4), calls=%async_computation.5 | async-start | bytes 557056 | tf_op jit(solution)/shard_map/all_to_all | solution.py:432
Sparse Core Ops, SparseCore 0:
  13.1 28.6 all-gather.14
  43.3 101.9 all-gather.6
  147.8 27.3 all-gather.8
  177.4 55.9 all-gather.10
  235.8 55.9 all-gather.12
  312.9 71.2 reduce-scatter.8
  388.1 71.2 reduce-scatter.6
  462.9 51.0 reduce-scatter.4
  516.2 56.7 reduce-scatter.10
